TPU v7x, 128 devices: a whole 4x4x4 slice. The times are simulated.
128 devices in a mesh: ctx: 16 (over x_lo, y, core), fsdp: 8 (over z, x_hi).
Axes of the slice: x: 4 (x_hi: 2, x_lo: 2; x = x_hi * 2 + x_lo), y: 4, z: 4, core: 2. Of those that a mesh axis runs over, the one named last changes fastest.
Arguments:
- hidden_in: bfloat16 [8, 2048, 1024], P('fsdp', 'ctx'), may hold values from -6 to 6
- qkv_weight: bfloat16 [1024, 3072], P('fsdp'), may hold values from -0.1875 to 0.1875
- out_weight: bfloat16 [1024, 1024], P('fsdp'), may hold values from -4 to 4
- gate_up_weight: bfloat16 [1024, 5248], P('fsdp'), may hold values from -0.1875 to 0.1875
- down_weight: bfloat16 [2624, 1024], P('fsdp'), may hold values from -0.125 to 0.125
- attn_gain: bfloat16 [1024], P('fsdp'), may hold values from 0.5 to 1.5
- mlp_gain: bfloat16 [1024], P('fsdp'), may hold values from 0.5 to 1.5
- out_grad: bfloat16 [8, 2048, 1024], P('fsdp', 'ctx'), may hold values from -6 to 6
Outputs:
- result: bfloat16 [8, 2048, 1024], P('fsdp', 'ctx')
- input_grad: bfloat16 [8, 2048, 1024], P('fsdp', 'ctx')
- qkv_grad: float32 [1024, 3072], P('fsdp')
- out_weight_grad: float32 [1024, 1024], P('fsdp')
- gate_up_grad: float32 [1024, 5248], P('fsdp')
- down_grad: float32 [2624, 1024], P('fsdp')
- attn_gain_grad: float32 [1024], P('fsdp')
- mlp_gain_grad: float32 [1024], P('fsdp')
All inputs are finite; a program needn't handle non-finite values.
Results may differ from a plain program's by a relative error of at most 0.025.
Values may be sent and summed in bfloat16 or wider, within the bound.
A program may use at most 128 MiB of HBM per device.

v0:
```python
import jax
import jax.numpy as jnp
from jax import lax
from jax.sharding import PartitionSpec as P

HEADS = 16


EPSILON = 1e-05
ROPE_BASE = 160000.0


def rope_tables(positions, head_size):
    half_size = head_size // 2
    inverse = ROPE_BASE ** (-(jnp.arange(half_size, dtype=jnp.float32) * 2.0) / head_size)
    angles = positions.astype(jnp.float32)[:, None] * inverse[None, :]
    return (jnp.cos(angles)[:, None, :], jnp.sin(angles)[:, None, :])


def rotate_heads(values_in, cos_table, sin_table):
    half_size = values_in.shape[-1] // 2
    first = values_in[..., :half_size]
    second = values_in[..., half_size:]
    return jnp.concatenate(
        [first * cos_table - second * sin_table, second * cos_table + first * sin_table], axis=-1
    )


def unrotate_heads(grads_in, cos_table, sin_table):
    half_size = grads_in.shape[-1] // 2
    first = grads_in[..., :half_size]
    second = grads_in[..., half_size:]
    return jnp.concatenate(
        [first * cos_table + second * sin_table, second * cos_table - first * sin_table], axis=-1
    )


def layer_norm(values_in, gain):
    centered = values_in - jnp.mean(values_in, axis=-1, keepdims=True)
    inv_std = lax.rsqrt(jnp.mean(centered * centered, axis=-1, keepdims=True) + EPSILON)
    scaled = centered * inv_std
    return (scaled * gain, scaled, inv_std)


def norm_back(d_normed, scaled, inv_std, gain):
    d_gain = jnp.sum(d_normed * scaled, axis=0)
    d_scaled = d_normed * gain
    d_input = inv_std * (
        d_scaled
        - jnp.mean(d_scaled, axis=-1, keepdims=True)
        - scaled * jnp.mean(d_scaled * scaled, axis=-1, keepdims=True)
    )
    return (d_gain, d_input)


def to_groups(matrix, group_count, per_group, head_size):
    return matrix.reshape(matrix.shape[0], group_count, per_group, head_size).transpose(1, 0, 2, 3)


def from_groups(stacked):
    return stacked.transpose(1, 0, 2, 3).reshape(stacked.shape[1], -1)


def body(
    hidden_in, qkv_weight, out_weight, gate_up_weight, down_weight, attn_gain, mlp_gain, out_grad
):
    tok_rows = hidden_in.shape[1]
    model_width = hidden_in.shape[2]
    head_size = model_width // HEADS
    per_group = 4
    group_count = HEADS // per_group
    scale = head_size ** (-0.5)
    hidden = hidden_in[0].astype(jnp.float32)
    grad_bf = out_grad[0]
    grad_full = grad_bf.astype(jnp.float32)
    positions = lax.axis_index("ctx") * tok_rows + jnp.arange(tok_rows)
    cos_table, sin_table = rope_tables(positions, head_size)

    def attn_params():
        return (
            lax.all_gather(qkv_weight, "fsdp", axis=0, tiled=True),
            lax.all_gather(out_weight, "fsdp", axis=0, tiled=True),
            lax.all_gather(attn_gain, "fsdp", axis=0, tiled=True),
        )

    def mlp_params():
        return (
            lax.all_gather(gate_up_weight, "fsdp", axis=0, tiled=True),
            lax.all_gather(down_weight, "fsdp", axis=0, tiled=True),
            lax.all_gather(mlp_gain, "fsdp", axis=0, tiled=True),
        )

    def attend_group(block):
        query_g, key_g, value_g = block
        scores = (
            jnp.einsum("qhd,khd->hqk", query_g, key_g, preferred_element_type=jnp.float32) * scale
        )
        top_score = jnp.max(scores, axis=-1, keepdims=True)
        log_total = top_score[..., 0] + jnp.log(jnp.sum(jnp.exp(scores - top_score), axis=-1))
        weights_b = jnp.exp(scores - log_total[..., None]).astype(jnp.bfloat16)
        mixed = jnp.einsum("hqk,khd->qhd", weights_b, value_g, preferred_element_type=jnp.float32)
        return (mixed, log_total)

    w_qkv, w_out, gain_one = attn_params()
    gain_one = gain_one.astype(jnp.float32)
    normed_full, scaled_one, inv_one = layer_norm(hidden, gain_one)
    normed_one = normed_full.astype(jnp.bfloat16)
    projected = jnp.dot(normed_one, w_qkv, preferred_element_type=jnp.float32)
    queries = projected[:, :model_width].reshape(tok_rows, HEADS, head_size)
    keys_part = projected[:, model_width : 2 * model_width].reshape(tok_rows, HEADS, head_size)
    query_b = (
        rotate_heads(queries, cos_table, sin_table)
        .reshape(tok_rows, model_width)
        .astype(jnp.bfloat16)
    )
    key_b = (
        rotate_heads(keys_part, cos_table, sin_table)
        .reshape(tok_rows, model_width)
        .astype(jnp.bfloat16)
    )
    value_b = projected[:, 2 * model_width :].astype(jnp.bfloat16)
    all_keys, all_values = (
        lax.all_gather(key_b, "ctx", axis=0, tiled=True),
        lax.all_gather(value_b, "ctx", axis=0, tiled=True),
    )
    query_groups = to_groups(query_b, group_count, per_group, head_size)
    mixed_groups, log_totals = lax.map(
        attend_group,
        (
            query_groups,
            to_groups(all_keys, group_count, per_group, head_size),
            to_groups(all_values, group_count, per_group, head_size),
        ),
    )
    attended = from_groups(mixed_groups).astype(jnp.bfloat16)
    first_sum = hidden + jnp.dot(attended, w_out, preferred_element_type=jnp.float32)
    w_gate_up, w_down, gain_two = mlp_params()
    gain_two = gain_two.astype(jnp.float32)
    normed_two_full, scaled_two, inv_two = layer_norm(first_sum, gain_two)
    normed_two = normed_two_full.astype(jnp.bfloat16)
    gate_up = jnp.dot(normed_two, w_gate_up, preferred_element_type=jnp.float32)
    hidden_units = w_down.shape[0]
    gate_part = gate_up[:, :hidden_units]
    up_part = gate_up[:, hidden_units:]
    normal_cdf = 0.5 * (1.0 + lax.erf(gate_part * 2.0 ** (-0.5)))
    gelu_value = gate_part * normal_cdf
    activated = (gelu_value * up_part).astype(jnp.bfloat16)
    result = (first_sum + jnp.dot(activated, w_down, preferred_element_type=jnp.float32)).astype(
        jnp.bfloat16
    )
    w_gate_up, w_down, gain_two = mlp_params()
    gain_two = gain_two.astype(jnp.float32)
    down_local = jnp.dot(activated.T, grad_bf, preferred_element_type=jnp.float32)
    d_activated = jnp.dot(grad_bf, w_down.T, preferred_element_type=jnp.float32)
    normal_pdf = jnp.exp(-0.5 * gate_part * gate_part) * (2.0 * jnp.pi) ** (-0.5)
    d_gate = d_activated * up_part * (normal_cdf + gate_part * normal_pdf)
    d_up = d_activated * gelu_value
    d_gate_up = jnp.concatenate([d_gate, d_up], axis=-1).astype(jnp.bfloat16)
    gate_up_local = jnp.dot(normed_two.T, d_gate_up, preferred_element_type=jnp.float32)
    d_normed_two = jnp.dot(d_gate_up, w_gate_up.T, preferred_element_type=jnp.float32)
    gain_two_local, d_first_norm = norm_back(d_normed_two, scaled_two, inv_two, gain_two)
    d_first_sum = grad_full + d_first_norm
    w_qkv, w_out, gain_one = attn_params()
    gain_one = gain_one.astype(jnp.float32)
    d_first_b = d_first_sum.astype(jnp.bfloat16)
    out_local = jnp.dot(attended.T, d_first_b, preferred_element_type=jnp.float32)
    d_attended = jnp.dot(d_first_b, w_out.T, preferred_element_type=jnp.float32).astype(
        jnp.bfloat16
    )
    back_keys, back_values = (all_keys, all_values)
    key_groups = to_groups(back_keys, group_count, per_group, head_size)
    value_groups = to_groups(back_values, group_count, per_group, head_size)
    dout_groups = to_groups(d_attended, group_count, per_group, head_size)

    def query_side(block):
        query_g, key_g, value_g, dout_g, log_total = block
        scores = (
            jnp.einsum("qhd,khd->hqk", query_g, key_g, preferred_element_type=jnp.float32) * scale
        )
        prob = jnp.exp(scores - log_total[..., None])
        d_prob = jnp.einsum("qhd,khd->hqk", dout_g, value_g, preferred_element_type=jnp.float32)
        delta = jnp.sum(prob * d_prob, axis=-1)
        d_scores = (prob * (d_prob - delta[..., None])).astype(jnp.bfloat16)
        d_query = (
            jnp.einsum("hqk,khd->qhd", d_scores, key_g, preferred_element_type=jnp.float32) * scale
        )
        return (d_query, delta, prob.astype(jnp.bfloat16), d_scores)

    def query_and_keys(block):
        query_g = block[0]
        dout_g = block[3]
        d_query, delta, prob_b, d_scores = query_side(block)
        d_key = (
            jnp.einsum("hqk,qhd->khd", d_scores, query_g, preferred_element_type=jnp.float32)
            * scale
        )
        d_value = jnp.einsum("hqk,qhd->khd", prob_b, dout_g, preferred_element_type=jnp.float32)
        return (d_query, d_key, d_value)

    d_query_groups, d_key_groups, d_value_groups = lax.map(
        query_and_keys, (query_groups, key_groups, value_groups, dout_groups, log_totals)
    )
    d_key_own, d_value_own = (
        lax.psum_scatter(
            from_groups(d_key_groups).astype(jnp.bfloat16), "ctx", scatter_dimension=0, tiled=True
        ).astype(jnp.float32),
        lax.psum_scatter(
            from_groups(d_value_groups).astype(jnp.bfloat16), "ctx", scatter_dimension=0, tiled=True
        ).astype(jnp.float32),
    )
    d_query = unrotate_heads(
        from_groups(d_query_groups).reshape(tok_rows, HEADS, head_size), cos_table, sin_table
    ).reshape(tok_rows, model_width)
    d_key = unrotate_heads(
        d_key_own.reshape(tok_rows, HEADS, head_size), cos_table, sin_table
    ).reshape(tok_rows, model_width)
    d_projected = jnp.concatenate([d_query, d_key, d_value_own], axis=-1).astype(jnp.bfloat16)
    qkv_local = jnp.dot(normed_one.T, d_projected, preferred_element_type=jnp.float32)
    d_normed_one = jnp.dot(d_projected, w_qkv.T, preferred_element_type=jnp.float32)
    gain_one_local, d_input_norm = norm_back(d_normed_one, scaled_one, inv_one, gain_one)
    input_grad = (d_first_sum + d_input_norm).astype(jnp.bfloat16)
    shard_sums = (
        lax.psum_scatter(
            qkv_local.astype(jnp.bfloat16), "fsdp", scatter_dimension=0, tiled=True
        ).astype(jnp.float32),
        lax.psum_scatter(
            out_local.astype(jnp.bfloat16), "fsdp", scatter_dimension=0, tiled=True
        ).astype(jnp.float32),
        lax.psum_scatter(
            gate_up_local.astype(jnp.bfloat16), "fsdp", scatter_dimension=0, tiled=True
        ).astype(jnp.float32),
        lax.psum_scatter(
            down_local.astype(jnp.bfloat16), "fsdp", scatter_dimension=0, tiled=True
        ).astype(jnp.float32),
        lax.psum_scatter(
            gain_one_local.astype(jnp.bfloat16), "fsdp", scatter_dimension=0, tiled=True
        ).astype(jnp.float32),
        lax.psum_scatter(
            gain_two_local.astype(jnp.bfloat16), "fsdp", scatter_dimension=0, tiled=True
        ).astype(jnp.float32),
    )
    totals = (
        lax.psum(shard_sums[0].astype(jnp.bfloat16), "ctx").astype(jnp.float32),
        lax.psum(shard_sums[1].astype(jnp.bfloat16), "ctx").astype(jnp.float32),
        lax.psum(shard_sums[2].astype(jnp.bfloat16), "ctx").astype(jnp.float32),
        lax.psum(shard_sums[3].astype(jnp.bfloat16), "ctx").astype(jnp.float32),
        lax.psum(shard_sums[4].astype(jnp.bfloat16), "ctx").astype(jnp.float32),
        lax.psum(shard_sums[5].astype(jnp.bfloat16), "ctx").astype(jnp.float32),
    )
    return (
        result[None],
        input_grad[None],
        totals[0],
        totals[1],
        totals[2],
        totals[3],
        totals[4],
        totals[5],
    )


def solution(mesh):
    return jax.shard_map(
        body,
        mesh=mesh,
        in_specs=(
            P("fsdp", "ctx", None),
            P("fsdp", None),
            P("fsdp", None),
            P("fsdp", None),
            P("fsdp", None),
            P("fsdp"),
            P("fsdp"),
            P("fsdp", "ctx", None),
        ),
        out_specs=(
            P("fsdp", "ctx", None),
            P("fsdp", "ctx", None),
            P("fsdp", None),
            P("fsdp", None),
            P("fsdp", None),
            P("fsdp", None),
            P("fsdp"),
            P("fsdp"),
        ),
        check_vma=False,
    )
```

profile of v0, /device:TPU:1, one launch (start us, length us, event | category | flops | bytes accessed | tf_op | source)
XLA Modules:
  0.0 1213.4 jit_solution(10146555584693266223)
XLA Ops:
  7.9 21.7 %all-gather = bf16[8,1,128]{2,1,0:T(2,128)(2,1)S(1)} all-gather(bf16[1,1,128]{2,1,0:T(2,128)(2,1)} %bitcast.242), channel_id=1, replica_groups=mesh['ctx'=16,'fsdp'=8] {'fsdp'}, dimensions={0}, use_global_device_ids=true | all-gather | bytes 2304 | tf_op jit(solution)/shard_map/all_gather | solution.py:83
  31.9 70.3 %all-gather.9.cloned.1.call-done = bf16[1024,3072]{1,0:T(8,128)(2,1)} async-done(((bf16[128,3072]{1,0:T(8,128)(2,1)}), bf16[1024,3072]{1,0:T(8,128)(2,1)}) %all-gather.9.cloned.1.call-update) | async-done | bytes 6291472 | tf_op jit(solution)/shard_map/all_gather | solution.py:81
  102.2 3.9 fusion.78
  110.4 15.2 %all-gather.1 = bf16[8,1,128]{2,1,0:T(2,128)(2,1)S(1)} all-gather(bf16[1,1,128]{2,1,0:T(2,128)(2,1)S(1)} %bitcast.243), channel_id=1, replica_groups=mesh['ctx'=16,'fsdp'=8] {'fsdp'}, dimensions={0}, use_global_device_ids=true | all-gather | bytes 2304 | tf_op jit(solution)/shard_map/all_gather | solution.py:90
  125.7 17.4 %all-gather.11.cloned.1.call-done = bf16[2048,1024]{1,0:T(8,128)(2,1)} async-done(((bf16[128,1024]{1,0:T(8,128)(2,1)}), bf16[2048,1024]{1,0:T(8,128)(2,1)}) %all-gather.11.cloned.1.call-update) | async-done | bytes 4194320 | tf_op jit(solution)/shard_map/all_gather | solution.py:124
  143.0 6.5 copy.33
  149.5 41.0 %all-gather.13.cloned.1.call-done = bf16[2048,1024]{0,1:T(8,128)(2,1)} async-done(((bf16[128,1024]{0,1:T(8,128)(2,1)}), bf16[2048,1024]{0,1:T(8,128)(2,1)}) %all-gather.13.cloned.1.call-update) | async-done | bytes 4194320 | tf_op jit(solution)/shard_map/all_gather | solution.py:123
  190.6 20.6 %while.28 = (s32[]{:T(128)}, bf16[4,128,4,64]{1,3,2,0:T(8,128)(2,1)S(1)}, f32[4,4,128]{2,1,0:T(4,128)S(1)}, bf16[4,2048,4,64]{1,3,2,0:T(8,128)(2,1)}, bf16[4,128...) while((s32[]{:T(128)}, bf16[4,128,4,64]{1,3,2,0:T(8,128)(2,1)S(1)}, ...), condition=%wide.region_5.6_spmd.clone, body=%wide.region_2.5_spmd.sunk.clone | while | flops 276823552 | bytes 14895185 | solution.py:127
  190.6 2.1 multiply_reduce_fusion.11
  193.5 2.2 fusion.126
  195.7 2.1 multiply_reduce_fusion.11
  198.6 2.2 fusion.126
  200.9 2.1 multiply_reduce_fusion.11
  203.8 2.2 fusion.126
  206.0 2.1 multiply_reduce_fusion.11
  208.9 2.2 fusion.126
  211.2 35.0 %all-gather.15.cloned.1.call-done = bf16[1024,1024]{1,0:T(8,128)(2,1)} async-done(((bf16[128,1024]{1,0:T(8,128)(2,1)}), bf16[1024,1024]{1,0:T(8,128)(2,1)}) %all-gather.15.cloned.1.call-update) | async-done | bytes 2097168 | tf_op jit(solution)/shard_map/all_gather | solution.py:82
  246.2 2.1 fusion.82
  248.6 126.1 %all-gather.17.cloned.1.call-done = bf16[1024,5248]{1,0:T(8,128)(2,1)} async-done(((bf16[128,5248]{1,0:T(8,128)(2,1)}), bf16[1024,5248]{1,0:T(8,128)(2,1)}) %all-gather.17.cloned.1.call-update) | async-done | bytes 10747920 | tf_op jit(solution)/shard_map/all_gather | solution.py:88
  374.7 5.7 fusion.80
  380.4 75.6 %all-gather.19.cloned.1.call-done = bf16[2624,1024]{1,0:T(8,128)(2,1)} async-done(((bf16[328,1024]{1,0:T(8,128)(2,1)}), bf16[2624,1024]{1,0:T(8,128)(2,1)}) %all-gather.19.cloned.1.call-update) | async-done | bytes 5373968 | tf_op jit(solution)/shard_map/all_gather | solution.py:89
  456.1 4.6 fusion.47
  460.7 8.3 multiply_reduce_fusion.2
  473.4 48.1 %while.29 = (s32[]{:T(128)}, f32[4,128,4,64]{1,3,2,0:T(8,128)}, bf16[4,2048,4,64]{1,3,2,0:T(8,128)(2,1)}, bf16[4,2048,4,64]{1,3,2,0:T(8,128)(2,1)}, bf16[4,2048,...) while((s32[]{:T(128)}, f32[4,128,4,64]{1,3,2,0:T(8,128)}, ...), condition=%wide.region_12.13_spmd.clone, body=%wide.region_10.12_spmd.sunk.clone | while | flops 680033792 | bytes 124140824 | solution.py:200
  473.4 2.2 fusion.135
  483.5 2.0 copy-done.10
  485.4 2.2 fusion.135
  493.1 2.0 fusion.137
  497.5 2.2 fusion.135
  509.5 2.2 fusion.135
  521.5 6.4 copy.40
  528.0 6.4 copy.42
  534.5 3.2 convolution_convert_fusion.3
  537.7 5.1 convolution_convert_fusion.1
  542.9 46.2 %reduce-scatter.19.cloned.1.call-done = bf16[128,1024]{1,0:T(8,128)(2,1)} async-done(((bf16[2048,1024]{1,0:T(8,128)(2,1)}), bf16[128,1024]{1,0:T(8,128)(2,1)}) %reduce-scatter.19.cloned.1.call-update) | async-done | bytes 262160
  592.7 64.1 %reduce-scatter.21.cloned.1.call-done = bf16[128,1024]{1,0:T(8,128)(2,1)} async-done(((bf16[2048,1024]{1,0:T(8,128)(2,1)}), bf16[128,1024]{1,0:T(8,128)(2,1)}) %reduce-scatter.21.cloned.1.call-update) | async-done | bytes 262160
  660.8 4.6 convolution_convert_fusion.2
  665.4 7.2 convolution_convert_fusion
  673.0 64.3 %reduce-scatter.13.cloned.1.call-done = bf16[128,1024]{1,0:T(8,128)(2,1)} async-done(((bf16[1024,1024]{1,0:T(8,128)(2,1)}), bf16[128,1024]{1,0:T(8,128)(2,1)}) %reduce-scatter.13.cloned.1.call-update) | async-done | bytes 262160 | tf_op jit(solution)/shard_map/reduce_scatter | solution.py:226
  737.2 95.4 %reduce-scatter.17.cloned.1.call-done = bf16[328,1024]{1,0:T(8,128)(2,1)} async-done(((bf16[2624,1024]{1,0:T(8,128)(2,1)}), bf16[328,1024]{1,0:T(8,128)(2,1)}) %reduce-scatter.17.cloned.1.call-update) | async-done | bytes 671760 | tf_op jit(solution)/shard_map/reduce_scatter | solution.py:232
  832.7 101.7 %reduce-scatter.11.cloned.1.call-done = bf16[128,3072]{1,0:T(8,128)(2,1)} async-done(((bf16[1024,3072]{1,0:T(8,128)(2,1)}), bf16[128,3072]{1,0:T(8,128)(2,1)}) %reduce-scatter.11.cloned.1.call-update) | async-done | bytes 786448 | tf_op jit(solution)/shard_map/reduce_scatter | solution.py:223
  934.3 137.8 %reduce-scatter.15.cloned.1.call-done = bf16[128,5248]{1,0:T(8,128)(2,1)} async-done(((bf16[1024,5248]{1,0:T(8,128)(2,1)}), bf16[128,5248]{1,0:T(8,128)(2,1)}) %reduce-scatter.15.cloned.1.call-update) | async-done | bytes 1343504 | tf_op jit(solution)/shard_map/reduce_scatter | solution.py:229
  1073.4 4.4 fusion.49
  1077.9 5.2 fusion.64
  1083.0 16.1 %all-reduce.4 = (bf16[1024]{0:T(1024)(128)(2,1)S(1)}, bf16[1024]{0:T(1024)(128)(2,1)S(1)}) all-reduce(bf16[1024]{0:T(1024)(128)(2,1)S(1)} %get-tuple-element.97, bf16[1024]{0:T(1024)(128)(2,1)S(1)} %get-tuple-element.95), channel_id=8, replica_groups=mesh['ctx'=16,'fsdp'=8] {'fsdp'}, use_global_device_ids=true, to_apply=%region_26.27.clone | all-reduce | flops 2048 | bytes 8192
  1099.3 31.6 %all-reduce.2 = (bf16[128]{0:T(256)(128)(2,1)S(1)}, bf16[128]{0:T(256)(128)(2,1)S(1)}) all-reduce(bf16[128]{0:T(256)(128)(2,1)S(1)} %dynamic-slice.1, bf16[128]{0:T(256)(128)(2,1)S(1)} %dynamic-slice.3), channel_id=1, replica_groups=mesh['ctx'=16,'fsdp'=8] {'ctx'}, use_global_device_ids=true, to_apply=%region_27.28 | all-reduce | flops 256 | bytes 1024 | tf_op jit(solution)/shard_map/psum | solution.py:247
  1132.8 66.8 %all-reduce.7.cloned.1.call-done = (bf16[128,3072]{1,0:T(8,128)(2,1)}, bf16[128,1024]{1,0:T(8,128)(2,1)}, bf16[128,5248]{1,0:T(8,128)(2,1)}, bf16[328,1024]{1,0:T(8,128)(2,1)}) async-done(((bf16[128,3072]{1,0:T(8,128)(2,1)}, bf16[128,1024]{1,0:T(8,128)(2,1)}, bf16[128,5248]{1,0:T(8,128)(2,1)}, bf16[328,1024]{1,0:T(8,128)(2,1)}), (bf16[128,3072]{1,0:T(8,128)(2,1)}, bf16[128,1024]{1,0:T(8,128)(2,1)}, ...) | async-done | bytes 3063824 | tf_op jit(solution)/shard_map/psum | solution.py:243
  1201.5 2.4 convert_element_type.168
  (187 shorter events, 66.3 us)
Async XLA Ops:
  7.2 95.0 %all-gather.9.cloned.1.call-start = ((), (), s32[]{:S(2)}) async-start(), calls=%async_computation.6 | async-start | bytes 7077888 | tf_op jit(solution)/shard_map/all_gather | solution.py:81
  7.9 135.1 %all-gather.11.cloned.1.call-start = ((), (), s32[]{:S(2)}) async-start(), calls=%async_computation.7 | async-start | bytes 4456448 | tf_op jit(solution)/shard_map/all_gather | solution.py:124
  106.9 83.6 %all-gather.13.cloned.1.call-start = ((), (), s32[]{:S(2)}) async-start(), calls=%async_computation.8 | async-start | bytes 4456448 | tf_op jit(solution)/shard_map/all_gather | solution.py:123
  107.5 2.9 copy-start.23
  108.6 137.6 %all-gather.15.cloned.1.call-start = ((), (), s32[]{:S(2)}) async-start(), calls=%async_computation.9 | async-start | bytes 2359296 | tf_op jit(solution)/shard_map/all_gather | solution.py:82
  109.2 265.5 %all-gather.17.cloned.1.call-start = ((), (), s32[]{:S(2)}) async-start(), calls=%async_computation.10 | async-start | bytes 12091392 | tf_op jit(solution)/shard_map/all_gather | solution.py:88
  109.7 346.3 %all-gather.19.cloned.1.call-start = ((), (), s32[]{:S(2)}) async-start(), calls=%async_computation.11 | async-start | bytes 6045696 | tf_op jit(solution)/shard_map/all_gather | solution.py:89
  110.3 478.8 %reduce-scatter.19.cloned.1.call-start = ((), (), s32[]{:S(2)}) async-start(), calls=%async_computation.16 | async-start | bytes 4456448
  190.6 55.6 %copy-start.1 = (bf16[1,128,1024]{2,1,0:T(8,128)(2,1)S(1)}, bf16[1,128,1024]{2,1,0:T(8,128)(2,1)}, u32[]{:S(2)}) copy-start(bf16[1,128,1024]{2,1,0:T(8,128)(2,1)} %param.12) | copy-start | bytes 786436
  211.2 35.0 %copy-start.5 = (bf16[4,128,4,64]{1,3,2,0:T(8,128)(2,1)}, bf16[4,128,4,64]{1,3,2,0:T(8,128)(2,1)S(1)}, u32[]{:S(2)}) copy-start(bf16[4,128,4,64]{1,3,2,0:T(8,128)(2,1)S(1)} %get-tuple-element.396) | copy-start | bytes 786436
  211.2 163.5 %copy-start.11 = (bf16[4,128,4,64]{1,3,2,0:T(8,128)(2,1)}, bf16[4,128,4,64]{1,3,2,0:T(8,128)(2,1)S(1)}, u32[]{:S(2)}) copy-start(bf16[4,128,4,64]{1,3,2,0:T(8,128)(2,1)S(1)} %get-tuple-element.90) | copy-start | bytes 786436
  460.7 8.3 copy-start.20
  460.7 8.3 copy-start.21
  460.7 8.3 copy-start.19
  460.7 9.4 copy-start.2
  473.4 2.5 copy-start
  473.4 2.6 copy-start.6
  477.4 2.2 copy-start.7
  479.6 3.4 copy-start.9
  481.0 2.4 copy-start.8
  485.4 2.5 copy-start
  485.4 2.6 copy-start.6
  489.4 2.2 copy-start.7
  491.6 3.4 copy-start.9
  493.0 2.4 copy-start.8
  497.5 2.5 copy-start
  497.5 2.6 copy-start.6
  501.5 2.2 copy-start.7
  503.7 3.4 copy-start.9
  505.1 2.4 copy-start.8
  509.5 2.5 copy-start
  509.5 2.6 copy-start.6
  515.7 3.4 copy-start.9
  517.1 2.4 copy-start.8
  527.9 128.8 %reduce-scatter.21.cloned.1.call-start = ((), (), s32[]{:S(2)}) async-start(), calls=%async_computation.17 | async-start | bytes 4456448
  534.4 202.8 %reduce-scatter.13.cloned.1.call-start = ((), (), s32[]{:S(2)}) async-start(), calls=%async_computation.13 | async-start | bytes 2359296 | tf_op jit(solution)/shard_map/reduce_scatter | solution.py:226
  537.7 295.0 %reduce-scatter.17.cloned.1.call-start = ((), (), s32[]{:S(2)}) async-start(), calls=%async_computation.15 | async-start | bytes 6045696 | tf_op jit(solution)/shard_map/reduce_scatter | solution.py:232
  542.8 391.5 %reduce-scatter.11.cloned.1.call-start = ((), (), s32[]{:S(2)}) async-start(), calls=%async_computation.12 | async-start | bytes 7077888 | tf_op jit(solution)/shard_map/reduce_scatter | solution.py:223
  658.5 2.2 copy-start.13
  665.4 406.7 %reduce-scatter.15.cloned.1.call-start = ((), (), s32[]{:S(2)}) async-start(), calls=%async_computation.14 | async-start | bytes 12091392 | tf_op jit(solution)/shard_map/reduce_scatter | solution.py:229
  672.6 399.5 %copy-start.24 = (u32[128]{0:T(128)S(1)}, u32[128]{0:T(128)}, u32[]{:S(2)}) copy-start(u32[128]{0:T(128)} %constant.89) | copy-start | bytes 1540
  672.7 526.9 %all-reduce.7.cloned.1.call-start = ((), (), s32[]{:S(2)}) async-start(), calls=%async_computation.18 | async-start | bytes 6127616 | tf_op jit(solution)/shard_map/psum | solution.py:243
  1073.4 4.5 copy-start.14
  1073.4 4.5 copy-start.16
  1073.4 4.5 copy-start.18
  1077.9 54.0 %copy-start.4 = (f32[128,1024]{1,0:T(8,128)S(1)}, f32[128,1024]{1,0:T(8,128)}, u32[]{:S(2)}) copy-start(f32[128,1024]{1,0:T(8,128)} %copy-done.3) | copy-start | bytes 1572868
  1199.6 4.4 copy-start.22
  1199.6 5.6 copy-start.12
  (8 other events, 12.4 us)
Sparse Core Ops, SparseCore 0:
  10.3 91.8 all-gather.8
  107.0 35.9 all-gather.10
  145.2 45.2 all-gather.12
  192.8 53.3 all-gather.14
  248.3 126.3 all-gather.16
  376.8 79.1 all-gather.18
  528.1 60.9 reduce-scatter.18
  591.5 65.2 reduce-scatter.20
  661.0 76.1 reduce-scatter.12
  740.9 91.6 reduce-scatter.16
  837.0 97.2 reduce-scatter.10
  938.5 133.5 reduce-scatter.14
  1074.9 124.6 all-reduce.6
where the time goes:
time: 1210 us
  waiting for transfers between devices  944 us (78%)
  matrix products  103 us (9%)
  blocking collectives  84.5 us (7%)
  local copies, waits for them, and re-layouts  44.8 us (4%)
  other arithmetic  21.4 us (2%)
  between operations  14.9 us (1%)
    reduce_scatter x1, waiting for transfers between devices, body(): lax.psum_scatter(gate_up_local.astype(jnp.bfloat16), 'fsdp', scatter_dime...  138 us
    all_gather x1, waiting for transfers between devices, mlp_params(): lax.all_gather(gate_up_weight, 'fsdp', axis=0, tiled=True)  126 us
    unnamed x15, waiting for transfers between devices  113 us
    reduce_scatter x1, waiting for transfers between devices, body(): lax.psum_scatter(qkv_local.astype(jnp.bfloat16), 'fsdp', scatter_dimensio...  102 us
    reduce_scatter x1, waiting for transfers between devices, body(): lax.psum_scatter(down_local.astype(jnp.bfloat16), 'fsdp', scatter_dimensi...  95.4 us
    all_gather x1, waiting for transfers between devices, mlp_params(): lax.all_gather(down_weight, 'fsdp', axis=0, tiled=True)  75.6 us
    all_gather x1, waiting for transfers between devices, attn_params(): lax.all_gather(qkv_weight, 'fsdp', axis=0, tiled=True)  70.3 us
    psum x1, waiting for transfers between devices, body(): lax.psum(shard_sums[0].astype(jnp.bfloat16), 'ctx').astype(jnp.float32)  66.8 us
  transfers between devices with their start and end apart: 13, of which 13 were waited for; matrix products, arithmetic and copies ran while one was open for 7% of the time, Pallas kernels for 0%

commit v1 on v0

v1 whole, which is shorter than its diff:
```python
import jax
import jax.numpy as jnp
import numpy as np
from jax import lax
from jax.experimental import pallas as pl
from jax.experimental.pallas import tpu as pltpu
from jax.sharding import PartitionSpec as P

HEADS = 16
EPSILON = 1e-05
ROPE_BASE = 160000.0
F32 = jnp.float32
BF16 = jnp.bfloat16
MESH = pl.DeviceIdType.MESH
ANY = pl.BlockSpec(memory_space=pl.ANY)
VMEM = pl.BlockSpec(memory_space=pltpu.VMEM)
MIB = 1024 * 1024


class Place:
    def __init__(self):
        c = lax.axis_index("ctx")
        self.c = c
        self.f = lax.axis_index("fsdp")
        k = c % 2
        y = (c // 2) % 4
        xl = c // 8
        self.k = k

        def at(x, row):
            return x * 4 + row % 4

        ox = 1 - xl
        self.other = c + 1 - 2 * k
        self.chip = {
            "S": at(xl, y),
            "P": at(xl, y + 1),
            "M": at(xl, y + 3),
            "F": at(xl, y + 2),
            "X": at(ox, y),
            "XP": at(ox, y + 1),
            "XM": at(ox, y + 3),
            "XF": at(ox, y + 2),
        }

        self.same_core = {name: chip * 2 + k for name, chip in self.chip.items()}
        self.cross_core = {name: chip * 2 + 1 - k for name, chip in self.chip.items()}
        self.ring = [(c + d) % 16 for d in range(16)]
        z, xh = self.f // 2, self.f % 2
        self.twin = z * 2 + 1 - xh
        self.planes = [(z + d) % 4 * 2 + xh for d in range(4)]
        self.twin_planes = [(z + d) % 4 * 2 + 1 - xh for d in range(4)]
        self.fsdp_peers = [{"fsdp": i} for i in [self.twin] + self.planes[1:]]

    def same(self, name):
        return self.same_core[name]

    def cross(self, name):
        return self.cross_core[name]


def lanes_of(f):
    return pl.ds(pl.multiple_of(f * 128, 128), 128)


def on_ctx(index):
    return {"ctx": index}


def greet(peers):
    barrier = pltpu.get_barrier_semaphore()
    for peer in peers:
        pl.semaphore_signal(barrier, inc=1, device_id=peer, device_id_type=MESH)
    pl.semaphore_wait(barrier, len(peers))


class Links:
    def __init__(self, send, recv, peer, like=()):
        self.send, self.recv, self.peer = send, recv, peer
        self.like = {ref.shape: ref for ref in like}
        self.open = []

    def copy(self, i, src, dst, peer):
        return pltpu.make_async_remote_copy(
            src_ref=src, dst_ref=dst, send_sem=self.send.at[i], recv_sem=self.recv.at[i],
            device_id=peer, device_id_type=MESH,
        )

    def put(self, i, src, dst, peer):
        self.copy(i, src, dst, peer).start()
        self.open.append((i, self.like.get(src.shape, src)))

    def got(self, i, dst):
        self.copy(i, dst, dst, self.peer).wait_recv()

    def close(self):
        for i, ref in self.open:
            self.copy(i, ref, ref, self.peer).wait_send()
        self.open = []


def ctx_peers(p):
    return [on_ctx(p.other), on_ctx(p.same("P")), on_ctx(p.same("M")), on_ctx(p.same("X"))]


GATHER_COPIES = 19


def gather_ctx(p, links, base, own, out, rows):
    half = rows // 2
    top, bottom = pl.ds(0, half), pl.ds(half, half)
    to_p, to_m, to_x, to_k = (
        on_ctx(p.same("P")), on_ctx(p.same("M")), on_ctx(p.same("X")), on_ctx(p.other),
    )
    mine = out.at[p.c]

    def put(i, src, dst, peer):
        links.put(base + i, src, dst, peer)

    def got(i, dst):
        links.got(base + i, dst)

    def block(name):
        return out.at[p.same(name)]

    def cross(name):
        return out.at[p.cross(name)]

    put(0, own, mine, to_p)
    put(1, own, mine, to_m)
    put(2, own, mine, to_x)
    put(3, own, mine, to_k)
    yield [p.same("S")]
    got(0, block("M"))
    put(4, block("M").at[top], block("M").at[top], to_p)
    put(10, block("M"), block("M"), to_k)
    got(1, block("P"))
    put(5, block("P").at[bottom], block("P").at[bottom], to_m)
    put(11, block("P"), block("P"), to_k)
    got(2, block("X"))
    put(6, block("X"), block("X"), to_p)
    put(7, block("X"), block("X"), to_m)
    put(12, block("X"), block("X"), to_k)
    got(3, cross("S"))
    yield [p.same("M"), p.same("P"), p.same("X"), p.cross("S")]
    for i, part, to_core in ((4, top, 13), (5, bottom, 14)):
        piece = block("F").at[part]
        got(i, piece)
        put(4 + i, piece, piece, to_x)
        put(to_core, piece, piece, to_k)
    got(10, cross("M"))
    got(11, cross("P"))
    yield [p.same("F"), p.cross("M"), p.cross("P")]
    got(6, block("XM"))
    put(15, block("XM"), block("XM"), to_k)
    got(7, block("XP"))
    put(16, block("XP"), block("XP"), to_k)
    got(12, cross("X"))
    got(13, cross("F").at[top])
    got(14, cross("F").at[bottom])
    yield [p.same("XM"), p.same("XP"), p.cross("X"), p.cross("F")]
    for i, part, to_core in ((8, top, 17), (9, bottom, 18)):
        piece = block("XF").at[part]
        got(i, piece)
        put(to_core, piece, piece, to_k)
    got(15, cross("XM"))
    got(16, cross("XP"))
    yield [p.same("XF"), p.cross("XM"), p.cross("XP")]
    got(17, cross("XF").at[top])
    got(18, cross("XF").at[bottom])
    yield [p.cross("XF")]


def gather_fsdp(p, links, base, own, slot):
    links.put(base, own, slot(p.f), {"fsdp": p.twin})
    for d in (1, 3, 2):
        links.put(base + d, own, slot(p.f), {"fsdp": p.planes[d]})
    yield []
    twin = slot(p.twin)
    links.got(base, twin)
    for d in (1, 3, 2):
        links.put(base + 3 + d, twin, twin, {"fsdp": p.planes[d]})
    yield [p.twin]
    for d in (1, 3, 2):
        links.got(base + d, slot(p.planes[4 - d]))
    for d in (1, 3, 2):
        links.got(base + 3 + d, slot(p.twin_planes[4 - d]))
    yield [p.planes[d] for d in (3, 1, 2)] + [p.twin_planes[d] for d in (3, 1, 2)]


def scatter_fsdp(p, links, base, part, along, across, keep, total, rows):
    for n, d in enumerate((1, 3, 2)):
        links.put(base + n, part(p.planes[d]), along.at[n], {"fsdp": p.planes[d]})
        links.put(base + 3 + n, part(p.twin_planes[d]), along.at[3 + n], {"fsdp": p.planes[d]})
    yield
    for n in range(6):
        links.got(base + n, along.at[n])
    terms = [(along.at[3 + n], 0) for n in range(3)]
    add_rows(across.at[0], [(part(p.twin), 0)] + terms, rows)
    links.put(base + 6, across.at[0], across.at[1], {"fsdp": p.twin})
    add_rows(keep, [(part(p.f), 0)] + [(along.at[n], 0) for n in range(3)], rows)
    yield
    links.got(base + 6, across.at[1])
    add_rows(total, [(keep, 0), (across.at[1], 0)], rows)


def run_all(stages):
    live = list(stages)
    while live:
        left = []
        for stage in live:
            try:
                next(stage)
                left.append(stage)
            except StopIteration:
                pass
        live = left


SCATTER_COPIES = 16
SCATTER_ORDER = ("XF", "XP", "XM", "F", "X", "P", "M", "S")


def add_rows(dst, terms, rows, at=0):
    step = 16

    def one(i, _):
        r = pl.multiple_of(i * step, step)
        total = None
        for ref, off in terms:
            part = ref[pl.ds(r + off, step), :].astype(F32)
            total = part if total is None else total + part
        dst[pl.ds(r + at, step), :] = total.astype(dst.dtype)
        return 0

    lax.fori_loop(0, rows // step, one, 0)


def scatter_ctx(p, links, base, part, total, core_in, mid, far, rows):
    half = rows // 2
    to_p, to_m, to_x, to_k = (
        on_ctx(p.same("P")), on_ctx(p.same("M")), on_ctx(p.same("X")), on_ctx(p.other),
    )

    def put(i, src, dst, peer):
        links.put(base + i, src, dst, peer)

    def got(i, dst):
        links.got(base + i, dst)

    for i, name in enumerate(SCATTER_ORDER):
        put(i, part.at[p.cross(name)], core_in.at[i], to_k)
    yield

    def pair(i):
        got(i, core_in.at[i])
        return [(part.at[p.same(SCATTER_ORDER[i])], 0), (core_in.at[i], 0)]

    for i, peer in ((0, to_x), (1, to_p), (2, to_m)):
        add_rows(mid.at[i], pair(i), rows)
        put(8 + i, mid.at[i], far.at[i], peer)
    yield
    terms = pair(3)
    got(8, far.at[0])
    add_rows(mid.at[3], terms + [(far.at[0], 0)], rows)
    put(11, mid.at[3, pl.ds(0, half)], far.at[3, pl.ds(0, half)], to_p)
    put(12, mid.at[3, pl.ds(half, half)], far.at[3, pl.ds(half, half)], to_m)
    yield
    terms = pair(4)
    got(9, far.at[1])
    got(10, far.at[2])
    add_rows(mid.at[4], terms + [(far.at[1], 0), (far.at[2], 0)], rows)
    put(13, mid.at[4], far.at[4], to_x)
    yield
    terms = pair(5)
    got(11, far.at[3, pl.ds(0, half)])
    add_rows(mid.at[5], terms + [(far.at[3], 0)], half)
    add_rows(mid.at[5], [(r, half) for r, _ in terms], half, half)
    put(14, mid.at[5], far.at[5], to_p)
    terms = pair(6)
    got(12, far.at[3, pl.ds(half, half)])
    add_rows(mid.at[6], terms, half)
    add_rows(mid.at[6], [(r, half) for r, _ in terms] + [(far.at[3], half)], half, half)
    put(15, mid.at[6], far.at[6], to_m)
    yield
    terms = pair(7)
    got(13, far.at[4])
    got(14, far.at[5])
    got(15, far.at[6])
    add_rows(total, terms + [(far.at[4], 0), (far.at[5], 0), (far.at[6], 0)], rows)


def scatter_scratch(rows, cols):
    return [
        pltpu.VMEM((8, rows, cols), BF16),
        pltpu.VMEM((7, rows, cols), BF16),
        pltpu.VMEM((7, rows, cols), BF16),
    ]


def dma(n):
    return pltpu.SemaphoreType.DMA((n,))


def params(cid, mib=60):
    return pltpu.CompilerParams(
        collective_id=cid, has_side_effects=True, vmem_limit_bytes=mib * MIB
    )


Q_BLOCK = 256


def pick_rows(select, matrix):
    return nt(select.astype(BF16), matrix).astype(BF16)


def ones_at(rows, cols, shift, valid):
    row = lax.broadcasted_iota(jnp.int32, (rows, cols), 0)
    col = lax.broadcasted_iota(jnp.int32, (rows, cols), 1)
    return jnp.where((col == row + shift) & (row < valid), 1.0, 0.0)


def unit_of(row, c):
    shard = sum(((row >= 21 * n).astype(jnp.int32) for n in range(1, 8)), 0)
    place = row - 21 * shard
    inside = (row < 168) & ((place < 20) | (c < 8))
    return jnp.where(inside, 328 * shard + 16 * place + c, -1)


def iota(dims, axis):
    return lax.broadcasted_iota(jnp.int32, dims, axis)


def forward_kernel(
    h_ref, dy_ref, wqkv_ref, wout_ref, wgu_ref, wdown_ref, g1_ref, g2_ref, cos_ref, sin_ref,
    att_ref, dyall_ref, wq_ref, gu_ref, woutall_ref, downall_ref, n1_ref,
    qt_ref, kt_ref, vt_ref, qr_ref, kr_ref, vr_ref, ot_ref, lse_ref,
    hall, n1, qkv_win, gu_acc, qkv_cols, gu_cols, down_rows, ob, send, recv, local,
):
    p = Place()
    links = Links(
        send, recv, on_ctx(p.other),
        [hall.at[0], hall.at[0, pl.ds(0, 64)], qkv_cols, gu_cols, down_rows,
         ob.at[:, pl.ds(0, 128)]],
    )
    wins = [
        pltpu.make_async_copy(
            wqkv_ref.at[:, pl.ds(pl.multiple_of(part * 1024 + (p.c // 2) * 128, 128), 128)],
            qkv_win.at[part], local.at[part],
        )
        for part in range(3)
    ]
    own_h = pltpu.make_async_copy(h_ref, hall.at[p.c], local.at[5])
    for copy in wins:
        copy.start()
    own_h.start()
    for i in range(3):
        wins[i].wait()
        qkv_cols[pl.ds(64 * i, 64), :] = pick_rows(
            ones_at(64, 128, (p.c % 2) * 64, 64), qkv_win[i]
        )
    row = iota((16, 128), 0)
    gains = jnp.where(row == 0, g1_ref[...].astype(F32), 0.0)
    gains = jnp.where(row == 1, g2_ref[...].astype(F32), gains)
    qkv_cols[pl.ds(192, 16), :] = gains.astype(BF16)
    greet([on_ctx(p.ring[d]) for d in range(1, 16)] + p.fsdp_peers)
    gather_wq = gather_fsdp(p, links, 38, qkv_cols, lambda f: wq_ref.at[:, lanes_of(f)])
    next(gather_wq)
    gather_h = gather_ctx(p, links, 0, h_ref, hall, 128)
    ready = next(gather_h)
    lanes = lanes_of(p.f)
    wq_ref[:, lanes] = qkv_cols[...]
    for half in range(2):
        want = unit_of(iota((176, 1), 0), p.c)
        want = jnp.where(want < 0, -1, want + 64 * half)
        gu_acc[...] = jnp.zeros_like(gu_acc)

        def pick(i, _):
            cols = pl.ds(pl.multiple_of(2560 * half + i * 896, 128), 896)
            select = jnp.where(iota((176, 896), 1) + i * 896 == want, 1.0, 0.0)
            gu_acc[...] += nt(select.astype(BF16), wgu_ref[:, cols])
            return 0

        lax.fori_loop(0, 3, pick, 0)
        gu_cols[pl.ds(176 * half, 176), :] = gu_acc[...].astype(BF16)
    place = iota((32, 328), 0)
    select = (iota((32, 328), 1) == 16 * place + p.c) & (place < 21)
    down_rows[...] = nn(jnp.where(select, 1.0, 0.0).astype(BF16), wdown_ref[...]).astype(BF16)
    own_h.wait()
    next(gather_wq)
    ready += next(gather_h)
    next(gather_wq)
    saves = []

    def project(b):
        gain = wq_ref[pl.ds(192, 1), :].astype(F32)

        def norm(i, _):
            r = pl.ds(pl.multiple_of(i * 32, 32), 32)
            xhat, _unused = normalize(hall[b, r, :].astype(F32))
            n1[b, r, :] = (xhat * gain).astype(BF16)
            return 0

        lax.fori_loop(0, 4, norm, 0)
        proj = nt(wq_ref[pl.ds(0, 192), :], n1[b])
        at = pl.ds(pl.multiple_of(b * 128, 128), 128)
        cos, sin = cos_ref[:, at], sin_ref[:, at]
        q = rope_t(proj[:64], cos, sin).astype(BF16) * jnp.asarray(0.125, BF16)
        k = rope_t(proj[64:128], cos, sin).astype(BF16)
        v = proj[128:192].astype(BF16)
        qt_ref[:, at] = q
        kt_ref[:, at] = k
        vt_ref[:, at] = v
        qr_ref[at, :] = q.astype(F32).T.astype(BF16)
        kr_ref[at, :] = k.astype(F32).T.astype(BF16)
        vr_ref[at, :] = v.astype(F32).T.astype(BF16)
        copy = pltpu.make_async_copy(n1.at[b], n1_ref.at[b], local.at[10 + len(saves)])
        copy.start()
        saves.append(copy)

    for b in ready:
        project(b)
    for b in next(gather_h):
        project(b)
    for b in next(gather_h):
        project(b)
    gather_gu = gather_fsdp(p, links, 45, gu_cols, lambda f: gu_ref.at[:, lanes_of(f)])
    next(gather_gu)
    def down_slot(f):
        return downall_ref.at[pl.ds(pl.multiple_of(f * 32, 32), 32)]

    gather_down = gather_fsdp(p, links, 83, down_rows, down_slot)
    next(gather_down)
    locals_ = [
        pltpu.make_async_copy(dy_ref, dyall_ref.at[p.c], local.at[6]),
        pltpu.make_async_copy(gu_cols, gu_ref.at[:, lanes], local.at[7]),
        pltpu.make_async_copy(
            wout_ref, woutall_ref.at[pl.ds(pl.multiple_of(p.f * 128, 128), 128)], local.at[8]
        ),
        pltpu.make_async_copy(down_rows, down_slot(p.f), local.at[3]),
    ]
    for copy in locals_:
        copy.start()
    half = pl.ds(pl.multiple_of(p.k * 64, 64), 64)

    def out_half(f, k):
        return woutall_ref.at[pl.ds(pl.multiple_of(f * 128 + k * 64, 64), 64)]

    gather_out = gather_fsdp(p, links, 53, wout_ref.at[half], lambda f: out_half(f, p.k))
    next(gather_out)
    while ready is not None:
        ready = next(gather_h, None)
        for b in ready or ():
            project(b)
    next(gather_gu)
    next(gather_down)
    twins = next(gather_out)
    gather_dy = gather_ctx(p, links, 19, dy_ref, dyall_ref, 128)
    next(gather_dy)
    stages = 6

    def attend(i, _):
        j = (p.c // 2 + i) % 8
        at = pl.ds(pl.multiple_of(j * Q_BLOCK, Q_BLOCK), Q_BLOCK)
        scores = nn(kr_ref[...], qt_ref[:, at])
        top = jnp.max(scores, axis=0, keepdims=True)
        weights = jnp.exp(scores - top)
        total = jnp.sum(weights, axis=0, keepdims=True)
        mixed = nn(vt_ref[...], weights.astype(BF16)) / total
        ot_ref[:, at] = mixed
        lse_ref[:, at] = top + jnp.log(total)
        ob[:, at] = mixed.astype(BF16)

        @pl.when(i > 0)
        def _():
            for e in range(2):
                to = 2 * j + e
                piece = ob.at[:, pl.ds(pl.multiple_of(to * 128, 128), 128)]
                links.copy(67 + 2 * i + e - p.k, piece, att_ref.at[p.c], on_ctx(to)).start()

        @pl.when(i == 0)
        def _():
            piece = ob.at[:, pl.ds(pl.multiple_of(p.c * 128, 128), 128)]
            copy = pltpu.make_async_copy(piece, att_ref.at[p.c], local.at[9])
            copy.start()
            copy.wait()
            piece = ob.at[:, pl.ds(pl.multiple_of(p.other * 128, 128), 128)]
            links.copy(67 + (p.other - p.c + 16) % 16, piece, att_ref.at[p.c], on_ctx(p.other)).start()

        for s in range(stages):

            @pl.when(i == s + 2)
            def _():
                next(gather_dy, None)

        return 0

    lax.fori_loop(0, 8, attend, 0)
    for _ in gather_dy:
        pass
    next(gather_gu)
    next(gather_down)
    others = twins + next(gather_out)
    for i, f in enumerate(others):
        links.put(60 + i, out_half(f, p.k), out_half(f, p.k), on_ctx(p.other))
    for d in range(1, 16):
        links.got(67 + d, att_ref.at[p.ring[16 - d]])
        links.open.append((67 + d, ob.at[:, pl.ds(0, 128)]))
    for i, f in enumerate(others):
        links.got(60 + i, out_half(f, 1 - p.k))

    for copy in locals_ + saves:
        copy.wait()
    links.close()


def shape(dims, dtype=BF16):
    return jax.ShapeDtypeStruct(dims, dtype)


def forward(hidden, grad, wqkv, wout, wgu, wdown, g1, g2, cos, sin):
    return pl.pallas_call(
        forward_kernel,
        name="forward",
        out_shape=(
            shape((16, 64, 128)), shape((16, 128, 1024)), shape((208, 1024)), shape((352, 1024)),
            shape((1024, 1024)), shape((256, 1024)), shape((16, 128, 1024)),
            shape((64, 2048)), shape((64, 2048)), shape((64, 2048)),
            shape((2048, 64)), shape((2048, 64)), shape((2048, 64)),
            shape((64, 2048), F32), shape((1, 2048), F32),
        ),
        in_specs=[VMEM, VMEM, ANY] + [VMEM] * 7,
        out_specs=(ANY, ANY, VMEM, ANY, ANY, ANY, ANY) + (VMEM,) * 8,
        scratch_shapes=[
            pltpu.VMEM((16, 128, 1024), BF16),
            pltpu.VMEM((16, 128, 1024), BF16),
            pltpu.VMEM((3, 128, 128), BF16),
            pltpu.VMEM((176, 128), F32),
            pltpu.VMEM((208, 128), BF16),
            pltpu.VMEM((352, 128), BF16),
            pltpu.VMEM((32, 1024), BF16),
            pltpu.VMEM((64, 2048), BF16),
            dma(90), dma(90), dma(26),
        ],
        compiler_params=params(1, 56),
    )(hidden, grad, wqkv, wout, wgu, wdown, g1, g2, cos, sin)


def middle_kernel(
    h_ref, att_ref, wout_ref, wq_ref, gu_ref, downall_ref, dy_ref, dyall_ref,
    h1_ref, dh1_ref, dot_ref, downpart_ref, ggu_ref, gdown_ref, ggain_ref, gout_ref,
    nall, dyall, act, dgu, down_w, part, downpart, total, core_in, mid, far, dat,
    send, recv, local,
):
    p = Place()
    links = Links(send, recv, on_ctx(p.other))
    load = pltpu.make_async_copy(dyall_ref, dyall, local.at[0])
    load.start()
    peers = [on_ctx(p.ring[d]) for d in range(1, 16)]
    greet(peers)
    gain = wq_ref[pl.ds(193, 1), :].astype(F32)
    att = att_ref[...].reshape(1024, 128)
    h1 = h_ref[...].astype(F32) + tn(att, wout_ref[...])
    h1_ref[...] = h1
    xhat, _unused = normalize(h1)
    nall[p.c] = (xhat * gain).astype(BF16)
    gather = gather_ctx(p, links, 0, nall.at[p.c], nall, 128)
    ready = next(gather)
    pick = iota((176, 256), 1)
    row = iota((176, 1), 0)
    shard = sum(((row >= 21 * n).astype(jnp.int32) for n in range(1, 8)), 0)
    want = jnp.where(row < 168, row + 11 * shard, -1)
    down_w[...] = nn(jnp.where(pick == want, 1.0, 0.0).astype(BF16), downall_ref[...]).astype(BF16)
    load.wait()

    def feed(b):
        n2 = nall[b]
        gu = nt(gu_ref[...], n2)
        d_act = nt(down_w[...], dyall[b])
        gate, up = gu[:176], gu[176:]
        cdf = 0.5 * (1.0 + lax.erf(gate * 2.0 ** (-0.5)))
        gelu = gate * cdf
        pdf = jnp.exp(-0.5 * gate * gate) * (2.0 * np.pi) ** (-0.5)
        d_gate = d_act * up * (cdf + gate * pdf)
        d_gu = jnp.concatenate([d_gate, d_act * gelu], axis=0).astype(BF16)
        at = pl.ds(pl.multiple_of(b * 128, 128), 128)
        act[:, at] = (gelu * up).astype(BF16)
        dgu[:, at] = d_gu
        part[b] = tn(d_gu, gu_ref[...]).astype(BF16)

    while ready is not None:
        for b in ready:
            feed(b)
        ready = next(gather, None)
    scatter = scatter_ctx(p, links, 19, part, total, core_in, mid, far, 128)
    next(scatter)
    next(scatter)
    ggain = []
    for half in range(2):
        cols = pl.ds(512 * half, 512)
        g = nn(dgu[...], nall[:, :, cols].reshape(2048, 512))
        ggu_ref[:, cols] = g.astype(BF16)
        ggain.append(jnp.sum(g * gu_ref[:, cols].astype(F32), axis=0, keepdims=True))
    ggain_ref[...] = jnp.concatenate(ggain, axis=1) / gain
    next(scatter)
    row = iota((256, 1), 0)
    shard = row // 32
    place = row - 32 * shard
    want = jnp.where(place < 21, 21 * shard + place, -1)
    spread = jnp.where(iota((256, 176), 1) == want, 1.0, 0.0).astype(BF16)
    for half in range(2):
        cols = pl.ds(512 * half, 512)
        g = nn(act[...], dyall[:, :, cols].reshape(2048, 512)).astype(BF16)
        gdown_ref[:, cols] = nn(spread, g).astype(BF16)
    next(scatter)

    def down(b, _):
        at = pl.ds(pl.multiple_of(b * 128, 128), 128)
        downpart[b] = tn(act[:, at], down_w[...]).astype(BF16)
        return 0

    next(scatter)
    lax.fori_loop(0, 16, down, 0)
    store = pltpu.make_async_copy(downpart, downpart_ref, local.at[1])
    store.start()
    next(scatter, None)
    h1 = h1_ref[...]
    xhat, inv = normalize(h1)
    d_h1 = dy_ref[...].astype(F32) + norm_back(total[...], xhat, inv, gain)
    dh1_ref[...] = d_h1
    d_h1_b = d_h1.astype(BF16)
    dat[...] = nt(wout_ref[...], d_h1_b).astype(BF16).reshape(16, 64, 128)
    lanes = pl.ds(pl.multiple_of(p.c * 128, 128), 128)
    for d in range(1, 16):
        links.put(34 + d, dat.at[p.ring[d]], dot_ref.at[:, lanes], peers[d - 1])
    dot_ref[:, lanes] = dat[p.c]
    att = att_ref[...]
    for g in range(4):
        rows = att[4 * g : 4 * g + 4].reshape(256, 128)
        block = nn(rows, d_h1_b).reshape(2, 16, 8, 1024).transpose(1, 0, 2, 3)
        gout_ref[:, pl.ds(16 * g, 16), :] = block.reshape(16, 16, 1024).astype(BF16)
    for d in range(1, 16):
        links.got(34 + d, dot_ref.at[:, pl.ds(pl.multiple_of(p.ring[16 - d] * 128, 128), 128)])
    store.wait()
    links.close()


def middle(hidden, att, w_out, w_q, w_gu, down_all, grad, dy_all):
    return pl.pallas_call(
        middle_kernel,
        name="middle",
        out_shape=(
            shape((128, 1024), F32), shape((128, 1024), F32), shape((64, 2048)),
            shape((16, 128, 1024)), shape((352, 1024)), shape((256, 1024)),
            shape((1, 1024), F32), shape((16, 64, 1024)),
        ),
        in_specs=[VMEM] * 7 + [ANY],
        out_specs=(VMEM,) * 3 + (ANY,) + (VMEM,) * 4,
        scratch_shapes=[
            pltpu.VMEM((16, 128, 1024), BF16),
            pltpu.VMEM((16, 128, 1024), BF16),
            pltpu.VMEM((176, 2048), BF16),
            pltpu.VMEM((352, 2048), BF16),
            pltpu.VMEM((176, 1024), BF16),
            pltpu.VMEM((16, 128, 1024), BF16),
            pltpu.VMEM((16, 128, 1024), BF16),
            pltpu.VMEM((128, 1024), F32),
        ] + scatter_scratch(128, 1024) + [
            pltpu.VMEM((16, 64, 128), BF16),
            dma(50), dma(50), dma(2),
        ],
        compiler_params=params(2),
    )(hidden, att, w_out, w_q, w_gu, down_all, grad, dy_all)


LATE = 224


def backward_kernel(
    k_ref, v_ref, kt_ref, qt_ref, q_ref, dot_ref, ot_ref, lse_ref, cos_ref, sin_ref,
    n1_ref, wq_ref, h_ref, h1_ref, dh1_ref, downpart_ref, ggu_ref, gdown_ref, ggain_ref, gout_ref,
    result_ref, dinput_ref, gupieces_ref, rowpieces_ref, latepieces_ref,
    n1, downpart, dproj, dk, dv, part, late, rows_in,
    total, gout, gu_sum, row_sum, late_sum, *rest,
):
    (
        core_a, mid_a, far_a, core_b, mid_b, far_b, core_c, mid_c, far_c,
        gu_along, gu_across, gu_keep, row_along, row_across, row_keep,
        late_along, late_across, late_keep, send, recv, local,
    ) = rest
    p = Place()
    links = Links(
        send, recv, on_ctx(p.other),
        [part.at[0], part.at[0, pl.ds(0, 64)], part.at[0, pl.ds(0, 32)], gu_keep,
         gu_keep.at[pl.ds(0, 176)], late_keep, late_keep.at[pl.ds(0, LATE // 2)]],
    )
    loads = [
        pltpu.make_async_copy(downpart_ref, downpart, local.at[0]),
        pltpu.make_async_copy(n1_ref, n1, local.at[1]),
    ]
    for copy in loads:
        copy.start()
    greet(ctx_peers(p) + p.fsdp_peers)
    loads[0].wait()
    down = scatter_ctx(p, links, 0, downpart, total.at[0], core_a, mid_a, far_a, 128)
    next(down)
    sum_gu = scatter_fsdp(
        p, links, 48, lambda f: ggu_ref.at[:, lanes_of(f)], gu_along, gu_across, gu_keep, gu_sum, 352
    )
    next(sum_gu)
    sum_out = scatter_ctx(p, links, 16, gout_ref, gout, core_b, mid_b, far_b, 64)
    all_gu = gather_ctx(p, links, 69, gu_sum, gupieces_ref, 352)
    mine = [
        pltpu.make_async_copy(gu_sum, gupieces_ref.at[p.c], local.at[2]),
        pltpu.make_async_copy(row_sum, rowpieces_ref.at[p.c], local.at[3]),
        pltpu.make_async_copy(late_sum, latepieces_ref.at[p.c], local.at[4]),
    ]

    def begin_gu():
        next(sum_gu, None)
        next(all_gu)

    def step(stages):
        return lambda: next(stages, None)

    plan = {
        1: [step(down)], 2: [step(sum_out)], 3: [step(sum_gu)], 4: [step(down)],
        5: [step(down), begin_gu], 6: [step(down)], 7: [step(sum_out), step(all_gu)],
    }
    dk[...] = jnp.zeros_like(dk)
    dv[...] = jnp.zeros_like(dv)

    def attend(i, _):
        at = pl.ds(pl.multiple_of(i * Q_BLOCK, Q_BLOCK), Q_BLOCK)
        scores = nn(k_ref[...], qt_ref[:, at])
        prob = jnp.exp(scores - lse_ref[:, at])
        dout = dot_ref[:, at]
        d_prob = nn(v_ref[...], dout)
        delta = jnp.sum(dout.astype(F32) * ot_ref[:, at], axis=0, keepdims=True)
        d_scores = (prob * (d_prob - delta)).astype(BF16)
        d_query = nn(kt_ref[...], d_scores) * 0.125
        dproj[pl.ds(0, 64), at] = unrope_t(d_query, cos_ref[:, at], sin_ref[:, at]).astype(BF16)
        dk[...] += nn(d_scores, q_ref[at, :])
        dv[...] += nn(prob.astype(BF16), dout.astype(F32).T.astype(BF16))
        for n, steps in plan.items():

            @pl.when(i == n)
            def _():
                for run in steps:
                    run()

        return 0

    lax.fori_loop(0, 8, attend, 0)

    def project(b, _):
        at = pl.ds(pl.multiple_of(b * 128, 128), 128)
        d_key = unrope_t(dk[at, :].T, cos_ref[:, at], sin_ref[:, at])
        dproj[pl.ds(64, 64), at] = d_key.astype(BF16)
        dproj[pl.ds(128, 64), at] = dv[at, :].T.astype(BF16)
        part[b] = tn(dproj[:, at], wq_ref[pl.ds(0, 192), :]).astype(BF16)
        return 0

    lax.fori_loop(0, 16, project, 0)
    back = scatter_ctx(p, links, 32, part, total.at[1], core_c, mid_c, far_c, 128)
    next(back)
    next(back)
    next(down, None)
    result_ref[...] = (h1_ref[...] + total[0]).astype(BF16)
    loads[1].wait()
    gain = wq_ref[pl.ds(192, 1), :].astype(F32)
    late[...] = jnp.zeros_like(late)
    ggain = []
    for half in range(2):
        cols = pl.ds(512 * half, 512)
        g = nn(dproj[...], n1[:, :, cols].reshape(2048, 512))
        late[pl.ds(0, 192), cols] = g.astype(BF16)
        ggain.append(jnp.sum(g * wq_ref[pl.ds(0, 192), cols].astype(F32), axis=0, keepdims=True))
    gain_row = jnp.concatenate(ggain, axis=1) / gain
    row = iota((16, 1024), 0)
    gains = jnp.where(row == 0, gain_row, 0.0)
    late[pl.ds(192, 16), :] = jnp.where(row == 1, ggain_ref[...], gains).astype(BF16)
    sum_late = scatter_fsdp(
        p, links, 62, lambda f: late.at[:, lanes_of(f)],
        late_along, late_across, late_keep, late_sum, LATE,
    )
    next(sum_late)
    next(back)
    next(sum_out, None)
    next(all_gu, None)
    next(back)
    for _ in sum_out:
        pass
    for f in range(8):
        rows_in[f, pl.ds(0, 16), :] = gdown_ref[pl.ds(32 * f, 16), :]
        tail = gdown_ref[pl.ds(32 * f + 16, 16), :].astype(F32)[:8]
        outs = gout[pl.ds(8 * f, 8), :]
        rows_in[f, pl.ds(16, 16), :] = jnp.concatenate([tail, outs], axis=0).astype(BF16)
    sum_rows = scatter_fsdp(
        p, links, 55, lambda f: rows_in.at[f], row_along, row_across, row_keep, row_sum, 32
    )
    next(sum_rows)
    next(back)
    next(sum_late)
    next(all_gu, None)
    next(back, None)
    xhat, inv = normalize(h_ref[...].astype(F32))
    d_in = norm_back(total[1], xhat, inv, gain)
    dinput_ref[...] = (dh1_ref[...] + d_in).astype(BF16)
    next(sum_late, None)
    all_late = gather_ctx(p, links, 107, late_sum, latepieces_ref, LATE)
    next(all_late)
    next(sum_rows)
    next(sum_rows, None)
    all_rows = gather_ctx(p, links, 88, row_sum, rowpieces_ref, 32)
    next(all_rows)
    for copy in mine:
        copy.start()
    run_all([all_gu, all_late, all_rows])
    for copy in mine:
        copy.wait()
    links.close()


def backward(*args):
    return pl.pallas_call(
        backward_kernel,
        name="backward",
        out_shape=(
            shape((128, 1024)), shape((128, 1024)), shape((16, 352, 128)),
            shape((16, 32, 1024)), shape((16, LATE, 128)),
        ),
        in_specs=[VMEM] * 10 + [ANY] + [VMEM] * 4 + [ANY] + [VMEM] * 4,
        out_specs=(VMEM, VMEM, ANY, ANY, ANY),
        scratch_shapes=[
            pltpu.VMEM((16, 128, 1024), BF16),
            pltpu.VMEM((16, 128, 1024), BF16),
            pltpu.VMEM((192, 2048), BF16),
            pltpu.VMEM((2048, 64), F32),
            pltpu.VMEM((2048, 64), F32),
            pltpu.VMEM((16, 128, 1024), BF16),
            pltpu.VMEM((LATE, 1024), BF16),
            pltpu.VMEM((8, 32, 1024), BF16),
            pltpu.VMEM((2, 128, 1024), F32),
            pltpu.VMEM((64, 1024), F32),
            pltpu.VMEM((352, 128), BF16),
            pltpu.VMEM((32, 1024), BF16),
            pltpu.VMEM((LATE, 128), BF16),
        ] + scatter_scratch(128, 1024) + scatter_scratch(64, 1024) + scatter_scratch(128, 1024)
        + fsdp_scratch(352, 128) + fsdp_scratch(32, 1024) + fsdp_scratch(LATE, 128)
        + [dma(126), dma(126), dma(5)],
        compiler_params=params(3),
    )(*args)


def fsdp_scratch(rows, cols):
    return [
        pltpu.VMEM((6, rows, cols), BF16),
        pltpu.VMEM((2, rows, cols), BF16),
        pltpu.VMEM((rows, cols), BF16),
    ]


def nt(a, b):
    return lax.dot_general(a, b, (((1,), (1,)), ((), ())), preferred_element_type=F32)


def tn(a, b):
    return lax.dot_general(a, b, (((0,), (0,)), ((), ())), preferred_element_type=F32)


def nn(a, b):
    return jnp.dot(a, b, preferred_element_type=F32)


def normalize(v):
    centered = v - jnp.mean(v, axis=-1, keepdims=True)
    inv = lax.rsqrt(jnp.mean(centered * centered, axis=-1, keepdims=True) + EPSILON)
    return centered * inv, inv


def norm_back(e, xhat, inv, gain):
    eg = e * gain
    return inv * (
        eg - jnp.mean(eg, axis=-1, keepdims=True)
        - xhat * jnp.mean(eg * xhat, axis=-1, keepdims=True)
    )


def rope_t(v, cos, sin):
    a, b = v[:32], v[32:]
    return jnp.concatenate([a * cos - b * sin, b * cos + a * sin], axis=0)


def unrope_t(v, cos, sin):
    a, b = v[:32], v[32:]
    return jnp.concatenate([a * cos + b * sin, b * cos - a * sin], axis=0)


def rope_tables():
    inverse = np.float32(ROPE_BASE) ** (-(np.arange(32, dtype=np.float32) * 2.0) / 64)
    angles = inverse[:, None].astype(np.float32) * np.arange(2048, dtype=np.float32)[None, :]
    return np.cos(angles).astype(np.float32), np.sin(angles).astype(np.float32)


def body(
    hidden_in, qkv_weight, out_weight, gate_up_weight, down_weight, attn_gain, mlp_gain, out_grad
):
    hidden_b, grad_b = hidden_in[0], out_grad[0]
    cos, sin = rope_tables()
    cos, sin = jnp.asarray(cos), jnp.asarray(sin)
    (
        att_t, dy_all, w_q, w_gu, w_out, down_all, n1, q_t, k_t, v_t, queries, keys, values, o_t, lse
    ) = forward(
        hidden_b, grad_b, qkv_weight, out_weight, gate_up_weight, down_weight,
        attn_gain[None], mlp_gain[None], cos, sin,
    )
    h1, d_h1, do_t, down_part, g_gu, g_down, g_gain_two, g_out = middle(
        hidden_b, att_t, w_out, w_q, w_gu, down_all, grad_b, dy_all
    )
    result, input_grad, gu_pieces, row_pieces, late_pieces = backward(
        keys, values, k_t, q_t, queries, do_t, o_t, lse, cos, sin,
        n1, w_q, hidden_b, h1, d_h1, down_part, g_gu, g_down, g_gain_two, g_out,
    )
    late_pieces = late_pieces.astype(F32)
    qkv_grad = (
        late_pieces[:, :192].reshape(16, 3, 64, 128).transpose(3, 1, 0, 2).reshape(128, 3072)
    )
    gain_grads = jnp.sum(late_pieces[:, 192:194], axis=0)
    gate_up = gu_pieces.reshape(16, 2, 176, 128)[:, :, :168].transpose(1, 2, 0, 3)
    gate_up = gate_up.reshape(2, 8, 336, 128)[:, :, :328].reshape(5248, 128)
    gate_up_grad = gate_up.astype(F32).T
    down_grad = (
        row_pieces[:, :21].transpose(1, 0, 2).reshape(336, 1024)[:328].astype(F32)
    )
    out_weight_grad = row_pieces[:, 24:].reshape(128, 1024).astype(F32)
    return (
        result[None], input_grad[None], qkv_grad, out_weight_grad, gate_up_grad, down_grad,
        gain_grads[0], gain_grads[1],
    )


def solution(mesh):
    return jax.shard_map(
        body,
        mesh=mesh,
        in_specs=(
            P("fsdp", "ctx", None), P("fsdp", None), P("fsdp", None), P("fsdp", None),
            P("fsdp", None), P("fsdp"), P("fsdp"), P("fsdp", "ctx", None),
        ),
        out_specs=(
            P("fsdp", "ctx", None), P("fsdp", "ctx", None), P("fsdp", None), P("fsdp", None),
            P("fsdp", None), P("fsdp", None), P("fsdp"), P("fsdp"),
        ),
        check_vma=False,
    )
```

time: 1210 us -> 234 us (0.19)
  waiting for transfers between devices: 944 us -> 0 us
  Pallas kernels: 0 us -> 220 us
  matrix products: 103 us -> 0 us
  blocking collectives: 84.5 us -> 0 us
  local copies, waits for them, and re-layouts: 44.8 us -> 9.6 us
  other arithmetic: 21.4 us -> 3.47 us
  between operations: 14.9 us -> 0.75 us
    reduce_scatter x4 -> x0, waiting for transfers between devices: 399 us -> none  [the longest x1 138 us: body(): lax.psum_scatter(gate_up_local.astype(jnp.bfloat16), 'fsdp', scatter_dime...]
    all_gather x6 -> x0, waiting for transfers between devices: 365 us -> none  [the longest x1 126 us: mlp_params(): lax.all_gather(gate_up_weight, 'fsdp', axis=0, tiled=True)]
    pallas_call x0 -> x3, Pallas kernels: none -> 220 us  [the longest x1 87.5 us: backward(): pl.pallas_call(backward_kernel, name='backward', out_shape=(shape((128, 1...]
    unnamed x15 -> x0, waiting for transfers between devices: 113 us -> none
    dot_general x40 -> x0, matrix products: 103 us -> none  [the longest x4 8.87 us: attend_group(): jnp.einsum('hqk,khd->qhd', weights_b, value_g, preferred_element_type=jnp...]
    psum x1 -> x0, waiting for transfers between devices: 66.8 us -> none  [body(): lax.psum(shard_sums[0].astype(jnp.bfloat16), 'ctx').astype(jnp.float32)]
    all_gather x2 -> x0, blocking collectives: 36.9 us -> none  [the longest x1 21.7 us: attn_params(): lax.all_gather(attn_gain, 'fsdp', axis=0, tiled=True)]
    psum x1 -> x0, blocking collectives: 31.6 us -> none  [body(): lax.psum(shard_sums[4].astype(jnp.bfloat16), 'ctx').astype(jnp.float32)]
  transfers between devices with their start and end apart: 13 -> 0, of which waited for: 13 -> 0; matrix products, arithmetic and copies ran while one was open for 7% -> 0% of each run, Pallas kernels for 0% -> 0%
where the time goes in v1:
time: 234 us
  Pallas kernels  220 us (94%)
  local copies, waits for them, and re-layouts  9.6 us (4%)
  other arithmetic  3.47 us (1%)
    pallas_call x1, Pallas kernels, backward(): pl.pallas_call(backward_kernel, name='backward', out_shape=(shape((128, 1...  87.5 us
    pallas_call x1, Pallas kernels, forward(): pl.pallas_call(forward_kernel, name='forward', out_shape=(shape((16, 64,...  69.9 us
    pallas_call x1, Pallas kernels, middle(): pl.pallas_call(middle_kernel, name='middle', out_shape=(shape((128, 1024)...  62.8 us
    unnamed x13, local copies, waits for them, and re-layouts  5.86 us

profile of v1, /device:TPU:1, one launch (start us, length us, event | category | flops | bytes accessed | tf_op | source)
XLA Modules:
  0.0 233.9 jit_solution(11037333433653146435)
XLA Ops:
  0.6 69.9 %forward.1 = (bf16[16,64,128]{2,1,0:T(8,128)(2,1)}, bf16[16,128,1024]{2,1,0:T(8,128)(2,1)}, bf16[208,1024]{1,0:T(8,128)(2,1)}, bf16[352,1024]{1,0:T(8,128)(2,1)}...) custom-call(bf16[128,1024]{1,0:T(8,128)(2,1)} %bitcast.33, ...), custom_call_target="tpu_custom_call" | custom-call | tf_op jit(solution)/shard_map/forward/pallas_call | solution.py:523
  70.5 62.8 %middle.1 = (f32[128,1024]{1,0:T(8,128)}, f32[128,1024]{1,0:T(8,128)}, bf16[64,2048]{1,0:T(8,128)(2,1)}, bf16[16,128,1024]{2,1,0:T(8,128)(2,1)}, bf16[352,1024]{...) custom-call(bf16[128,1024]{1,0:T(8,128)(2,1)} %bitcast.34, ...), custom_call_target="tpu_custom_call" | custom-call | tf_op jit(solution)/shard_map/middle/pallas_call | solution.py:650
  133.3 87.5 %backward.1 = (bf16[128,1024]{1,0:T(8,128)(2,1)}, bf16[128,1024]{1,0:T(8,128)(2,1)}, bf16[16,352,128]{2,1,0:T(8,128)(2,1)}, bf16[16,32,1024]{2,1,0:T(8,128)(2,1)}, bf16[16,224,128]{2,1,0:T(8,128)(2,1)}) custom-call(bf16[2048,64]{1,0:T(8,128)(2,1)} %get-tuple-element.35.k_ref, bf16[2048,64]{1,0:T(8,128)(2,1)} %get-tuple-element.36.v_ref, ...), custom_call_target="tpu_custom_call" | custom-call | tf_op jit(solution)/shard_map/backward/pallas_call | solution.py:827
  220.8 1.8 bitcast_convert_fusion
  222.6 1.2 slice_bitcast_fusion
  223.8 0.0 copy-start.1
  223.8 0.4 copy.21
  224.2 1.2 slice_convert_fusion
  225.4 0.0 copy-done.1
  225.4 0.1 slice.37
  225.5 0.4 copy.24
  225.9 0.1 slice.38
  226.0 0.3 convert_bitcast_fusion
  226.2 2.3 copy.23
  228.5 1.3 slice.36
  229.8 0.2 copy.19
  230.0 0.0 copy-start
  230.0 1.6 copy.22
  231.6 0.0 copy-done
  231.6 0.0 copy-start.3
  231.6 0.0 copy-start.2
  231.6 0.2 convert_element_type.16
  231.8 0.5 slice_bitcast_fusion.1
  232.3 0.2 copy-done.3
  232.5 0.7 copy.27
  233.2 0.0 copy-done.2
  233.2 0.7 copy.28
  (1 shorter events, 0.0 us)
Async XLA Ops:
  223.8 1.6 copy-start.1
  230.0 1.6 copy-start
  231.6 1.0 copy-start.3
  231.6 1.7 copy-start.2

commit v2 on v1

--- a/solution.py
+++ b/solution.py
@@ -93,10 +93,11 @@
     def got(self, i, dst):
         self.copy(i, dst, dst, self.peer).wait_recv()
 
-    def close(self):
+    def close(self, below=1000):
         for i, ref in self.open:
-            self.copy(i, ref, ref, self.peer).wait_send()
-        self.open = []
+            if i < below:
+                self.copy(i, ref, ref, self.peer).wait_send()
+        self.open = [(i, ref) for i, ref in self.open if i >= below]
 
 
 def ctx_peers(p):
@@ -236,7 +237,7 @@
     lax.fori_loop(0, rows // step, one, 0)
 
 
-def scatter_ctx(p, links, base, part, total, core_in, mid, far, rows):
+def scatter_ctx(p, links, base, part, total, core_in, far, rows):
     half = rows // 2
     to_p, to_m, to_x, to_k = (
         on_ctx(p.same("P")), on_ctx(p.same("M")), on_ctx(p.same("X")), on_ctx(p.other),
@@ -248,40 +249,41 @@
     def got(i, dst):
         links.got(base + i, dst)
 
+    mid = [part.at[p.same(name)] for name in SCATTER_ORDER]
     for i, name in enumerate(SCATTER_ORDER):
         put(i, part.at[p.cross(name)], core_in.at[i], to_k)
     yield
 
     def pair(i):
         got(i, core_in.at[i])
-        return [(part.at[p.same(SCATTER_ORDER[i])], 0), (core_in.at[i], 0)]
+        return [(mid[i], 0), (core_in.at[i], 0)]
 
     for i, peer in ((0, to_x), (1, to_p), (2, to_m)):
-        add_rows(mid.at[i], pair(i), rows)
-        put(8 + i, mid.at[i], far.at[i], peer)
+        add_rows(mid[i], pair(i), rows)
+        put(8 + i, mid[i], far.at[i], peer)
     yield
     terms = pair(3)
     got(8, far.at[0])
-    add_rows(mid.at[3], terms + [(far.at[0], 0)], rows)
-    put(11, mid.at[3, pl.ds(0, half)], far.at[3, pl.ds(0, half)], to_p)
-    put(12, mid.at[3, pl.ds(half, half)], far.at[3, pl.ds(half, half)], to_m)
+    add_rows(mid[3], terms + [(far.at[0], 0)], rows)
+    put(11, mid[3].at[pl.ds(0, half)], far.at[3, pl.ds(0, half)], to_p)
+    put(12, mid[3].at[pl.ds(half, half)], far.at[3, pl.ds(half, half)], to_m)
     yield
     terms = pair(4)
     got(9, far.at[1])
     got(10, far.at[2])
-    add_rows(mid.at[4], terms + [(far.at[1], 0), (far.at[2], 0)], rows)
-    put(13, mid.at[4], far.at[4], to_x)
+    add_rows(mid[4], terms + [(far.at[1], 0), (far.at[2], 0)], rows)
+    put(13, mid[4], far.at[4], to_x)
     yield
     terms = pair(5)
     got(11, far.at[3, pl.ds(0, half)])
-    add_rows(mid.at[5], terms + [(far.at[3], 0)], half)
-    add_rows(mid.at[5], [(r, half) for r, _ in terms], half, half)
-    put(14, mid.at[5], far.at[5], to_p)
+    add_rows(mid[5], terms + [(far.at[3], 0)], half)
+    add_rows(mid[5], [(r, half) for r, _ in terms], half, half)
+    put(14, mid[5], far.at[5], to_p)
     terms = pair(6)
     got(12, far.at[3, pl.ds(half, half)])
-    add_rows(mid.at[6], terms, half)
-    add_rows(mid.at[6], [(r, half) for r, _ in terms] + [(far.at[3], half)], half, half)
-    put(15, mid.at[6], far.at[6], to_m)
+    add_rows(mid[6], terms, half)
+    add_rows(mid[6], [(r, half) for r, _ in terms] + [(far.at[3], half)], half, half)
+    put(15, mid[6], far.at[6], to_m)
     yield
     terms = pair(7)
     got(13, far.at[4])
@@ -294,7 +296,6 @@
     return [
         pltpu.VMEM((8, rows, cols), BF16),
         pltpu.VMEM((7, rows, cols), BF16),
-        pltpu.VMEM((7, rows, cols), BF16),
     ]
 
 
@@ -332,11 +333,13 @@
     return lax.broadcasted_iota(jnp.int32, dims, axis)
 
 
-def forward_kernel(
+def front_kernel(
     h_ref, dy_ref, wqkv_ref, wout_ref, wgu_ref, wdown_ref, g1_ref, g2_ref, cos_ref, sin_ref,
-    att_ref, dyall_ref, wq_ref, gu_ref, woutall_ref, downall_ref, n1_ref,
-    qt_ref, kt_ref, vt_ref, qr_ref, kr_ref, vr_ref, ot_ref, lse_ref,
-    hall, n1, qkv_win, gu_acc, qkv_cols, gu_cols, down_rows, ob, send, recv, local,
+    wq_ref, h1_ref, dh1_ref, dot_ref, ggu_ref, gdown_ref, ggain_ref, gout_ref,
+    n1_ref, downpart_ref, qt_out, kt_out, qr_out, kr_out, vr_out, ot_out, lse_out,
+    hall, n1, dyall, nall, part, qt_ref, kt_ref, vt_ref, qr_ref, kr_ref, vr_ref, ot_ref, lse_ref,
+    qkv_win, gu_acc, qkv_cols, gu_cols, down_rows, ob, att_ref, dat,
+    woutall, gu_ref, downall, down_w, act, dgu, total, core_in, far, send, recv, local,
 ):
     p = Place()
     links = Links(
@@ -391,6 +394,30 @@
     next(gather_wq)
     ready += next(gather_h)
     next(gather_wq)
+    gather_gu = gather_fsdp(p, links, 45, gu_cols, lambda f: gu_ref.at[:, lanes_of(f)])
+    next(gather_gu)
+    def down_slot(f):
+        return downall.at[pl.ds(pl.multiple_of(f * 32, 32), 32)]
+
+    gather_down = gather_fsdp(p, links, 83, down_rows, down_slot)
+    next(gather_down)
+    locals_ = [
+        pltpu.make_async_copy(dy_ref, dyall.at[p.c], local.at[6]),
+        pltpu.make_async_copy(
+            wout_ref, woutall.at[pl.ds(pl.multiple_of(p.f * 128, 128), 128)], local.at[8]
+        ),
+        pltpu.make_async_copy(down_rows, down_slot(p.f), local.at[3]),
+    ]
+    for copy in locals_:
+        copy.start()
+    gu_ref[:, lanes] = gu_cols[...]
+    half = pl.ds(pl.multiple_of(p.k * 64, 64), 64)
+
+    def out_half(f, k):
+        return woutall.at[pl.ds(pl.multiple_of(f * 128 + k * 64, 64), 64)]
+
+    gather_out = gather_fsdp(p, links, 53, wout_ref.at[half], lambda f: out_half(f, p.k))
+    next(gather_out)
     saves = []
 
     def project(b):
@@ -423,32 +450,11 @@
         project(b)
     for b in next(gather_h):
         project(b)
-    for b in next(gather_h):
+    ready = next(gather_h)
+    gather_dy = gather_ctx(p, links, 19, dy_ref, dyall, 128)
+    next(gather_dy)
+    for b in ready:
         project(b)
-    gather_gu = gather_fsdp(p, links, 45, gu_cols, lambda f: gu_ref.at[:, lanes_of(f)])
-    next(gather_gu)
-    def down_slot(f):
-        return downall_ref.at[pl.ds(pl.multiple_of(f * 32, 32), 32)]
-
-    gather_down = gather_fsdp(p, links, 83, down_rows, down_slot)
-    next(gather_down)
-    locals_ = [
-        pltpu.make_async_copy(dy_ref, dyall_ref.at[p.c], local.at[6]),
-        pltpu.make_async_copy(gu_cols, gu_ref.at[:, lanes], local.at[7]),
-        pltpu.make_async_copy(
-            wout_ref, woutall_ref.at[pl.ds(pl.multiple_of(p.f * 128, 128), 128)], local.at[8]
-        ),
-        pltpu.make_async_copy(down_rows, down_slot(p.f), local.at[3]),
-    ]
-    for copy in locals_:
-        copy.start()
-    half = pl.ds(pl.multiple_of(p.k * 64, 64), 64)
-
-    def out_half(f, k):
-        return woutall_ref.at[pl.ds(pl.multiple_of(f * 128 + k * 64, 64), 64)]
-
-    gather_out = gather_fsdp(p, links, 53, wout_ref.at[half], lambda f: out_half(f, p.k))
-    next(gather_out)
     while ready is not None:
         ready = next(gather_h, None)
         for b in ready or ():
@@ -456,9 +462,7 @@
     next(gather_gu)
     next(gather_down)
     twins = next(gather_out)
-    gather_dy = gather_ctx(p, links, 19, dy_ref, dyall_ref, 128)
-    next(gather_dy)
-    stages = 6
+    plan = {1: gather_dy, 3: gather_dy, 4: gather_out, 6: gather_dy}
 
     def attend(i, _):
         j = (p.c // 2 + i) % 8
@@ -488,91 +492,52 @@
             piece = ob.at[:, pl.ds(pl.multiple_of(p.other * 128, 128), 128)]
             links.copy(67 + (p.other - p.c + 16) % 16, piece, att_ref.at[p.c], on_ctx(p.other)).start()
 
-        for s in range(stages):
-
-            @pl.when(i == s + 2)
+        for s, stages in plan.items():
+
+            @pl.when(i == s)
             def _():
-                next(gather_dy, None)
+                next(stages)
 
         return 0
 
     lax.fori_loop(0, 8, attend, 0)
-    for _ in gather_dy:
-        pass
-    next(gather_gu)
-    next(gather_down)
-    others = twins + next(gather_out)
+    saves += [
+        pltpu.make_async_copy(src, dst, local.at[26 + n])
+        for n, (src, dst) in enumerate((
+            (qt_ref, qt_out), (kt_ref, kt_out), (qr_ref, qr_out), (kr_ref, kr_out),
+            (vr_ref, vr_out), (ot_ref, ot_out), (lse_ref, lse_out),
+        ))
+    ]
+    for copy in saves[16:]:
+        copy.start()
+    others = twins + [p.planes[d] for d in (3, 1, 2)] + [p.twin_planes[d] for d in (3, 1, 2)]
     for i, f in enumerate(others):
         links.put(60 + i, out_half(f, p.k), out_half(f, p.k), on_ctx(p.other))
     for d in range(1, 16):
         links.got(67 + d, att_ref.at[p.ring[16 - d]])
         links.open.append((67 + d, ob.at[:, pl.ds(0, 128)]))
+    for copy in locals_:
+        copy.wait()
     for i, f in enumerate(others):
         links.got(60 + i, out_half(f, 1 - p.k))
 
-    for copy in locals_ + saves:
-        copy.wait()
-    links.close()
-
-
-def shape(dims, dtype=BF16):
-    return jax.ShapeDtypeStruct(dims, dtype)
-
-
-def forward(hidden, grad, wqkv, wout, wgu, wdown, g1, g2, cos, sin):
-    return pl.pallas_call(
-        forward_kernel,
-        name="forward",
-        out_shape=(
-            shape((16, 64, 128)), shape((16, 128, 1024)), shape((208, 1024)), shape((352, 1024)),
-            shape((1024, 1024)), shape((256, 1024)), shape((16, 128, 1024)),
-            shape((64, 2048)), shape((64, 2048)), shape((64, 2048)),
-            shape((2048, 64)), shape((2048, 64)), shape((2048, 64)),
-            shape((64, 2048), F32), shape((1, 2048), F32),
-        ),
-        in_specs=[VMEM, VMEM, ANY] + [VMEM] * 7,
-        out_specs=(ANY, ANY, VMEM, ANY, ANY, ANY, ANY) + (VMEM,) * 8,
-        scratch_shapes=[
-            pltpu.VMEM((16, 128, 1024), BF16),
-            pltpu.VMEM((16, 128, 1024), BF16),
-            pltpu.VMEM((3, 128, 128), BF16),
-            pltpu.VMEM((176, 128), F32),
-            pltpu.VMEM((208, 128), BF16),
-            pltpu.VMEM((352, 128), BF16),
-            pltpu.VMEM((32, 1024), BF16),
-            pltpu.VMEM((64, 2048), BF16),
-            dma(90), dma(90), dma(26),
-        ],
-        compiler_params=params(1, 56),
-    )(hidden, grad, wqkv, wout, wgu, wdown, g1, g2, cos, sin)
-
-
-def middle_kernel(
-    h_ref, att_ref, wout_ref, wq_ref, gu_ref, downall_ref, dy_ref, dyall_ref,
-    h1_ref, dh1_ref, dot_ref, downpart_ref, ggu_ref, gdown_ref, ggain_ref, gout_ref,
-    nall, dyall, act, dgu, down_w, part, downpart, total, core_in, mid, far, dat,
-    send, recv, local,
-):
-    p = Place()
-    links = Links(send, recv, on_ctx(p.other))
-    load = pltpu.make_async_copy(dyall_ref, dyall, local.at[0])
-    load.start()
-    peers = [on_ctx(p.ring[d]) for d in range(1, 16)]
-    greet(peers)
     gain = wq_ref[pl.ds(193, 1), :].astype(F32)
     att = att_ref[...].reshape(1024, 128)
-    h1 = h_ref[...].astype(F32) + tn(att, wout_ref[...])
+    h1 = h_ref[...].astype(F32) + tn(att, woutall[...])
     h1_ref[...] = h1
     xhat, _unused = normalize(h1)
     nall[p.c] = (xhat * gain).astype(BF16)
-    gather = gather_ctx(p, links, 0, nall.at[p.c], nall, 128)
+    gather = gather_ctx(p, links, 90, nall.at[p.c], nall, 128)
     ready = next(gather)
+    next(gather_gu)
+    next(gather_down)
     pick = iota((176, 256), 1)
     row = iota((176, 1), 0)
     shard = sum(((row >= 21 * n).astype(jnp.int32) for n in range(1, 8)), 0)
     want = jnp.where(row < 168, row + 11 * shard, -1)
-    down_w[...] = nn(jnp.where(pick == want, 1.0, 0.0).astype(BF16), downall_ref[...]).astype(BF16)
-    load.wait()
+    down_w[...] = nn(jnp.where(pick == want, 1.0, 0.0).astype(BF16), downall[...]).astype(BF16)
+    for _ in gather_dy:
+        pass
 
     def feed(b):
         n2 = nall[b]
@@ -593,7 +558,7 @@
         for b in ready:
             feed(b)
         ready = next(gather, None)
-    scatter = scatter_ctx(p, links, 19, part, total, core_in, mid, far, 128)
+    scatter = scatter_ctx(p, links, 109, part, total, core_in, far, 128)
     next(scatter)
     next(scatter)
     ggain = []
@@ -617,12 +582,13 @@
 
     def down(b, _):
         at = pl.ds(pl.multiple_of(b * 128, 128), 128)
-        downpart[b] = tn(act[:, at], down_w[...]).astype(BF16)
+        hall[b] = tn(act[:, at], down_w[...]).astype(BF16)
         return 0
 
     next(scatter)
+    links.close(90)
     lax.fori_loop(0, 16, down, 0)
-    store = pltpu.make_async_copy(downpart, downpart_ref, local.at[1])
+    store = pltpu.make_async_copy(hall, downpart_ref, local.at[4])
     store.start()
     next(scatter, None)
     h1 = h1_ref[...]
@@ -630,10 +596,10 @@
     d_h1 = dy_ref[...].astype(F32) + norm_back(total[...], xhat, inv, gain)
     dh1_ref[...] = d_h1
     d_h1_b = d_h1.astype(BF16)
-    dat[...] = nt(wout_ref[...], d_h1_b).astype(BF16).reshape(16, 64, 128)
+    dat[...] = nt(woutall[...], d_h1_b).astype(BF16).reshape(16, 64, 128)
     lanes = pl.ds(pl.multiple_of(p.c * 128, 128), 128)
     for d in range(1, 16):
-        links.put(34 + d, dat.at[p.ring[d]], dot_ref.at[:, lanes], peers[d - 1])
+        links.put(124 + d, dat.at[p.ring[d]], dot_ref.at[:, lanes], on_ctx(p.ring[d]))
     dot_ref[:, lanes] = dat[p.c]
     att = att_ref[...]
     for g in range(4):
@@ -641,37 +607,60 @@
         block = nn(rows, d_h1_b).reshape(2, 16, 8, 1024).transpose(1, 0, 2, 3)
         gout_ref[:, pl.ds(16 * g, 16), :] = block.reshape(16, 16, 1024).astype(BF16)
     for d in range(1, 16):
-        links.got(34 + d, dot_ref.at[:, pl.ds(pl.multiple_of(p.ring[16 - d] * 128, 128), 128)])
-    store.wait()
+        links.got(124 + d, dot_ref.at[:, pl.ds(pl.multiple_of(p.ring[16 - d] * 128, 128), 128)])
+    for copy in saves + [store]:
+        copy.wait()
     links.close()
 
 
-def middle(hidden, att, w_out, w_q, w_gu, down_all, grad, dy_all):
+def shape(dims, dtype=BF16):
+    return jax.ShapeDtypeStruct(dims, dtype)
+
+
+def front(hidden, grad, wqkv, wout, wgu, wdown, g1, g2, cos, sin):
+    heads = [
+        shape((64, 2048)), shape((64, 2048)), shape((2048, 64)), shape((2048, 64)),
+        shape((2048, 64)), shape((64, 2048), F32), shape((1, 2048), F32),
+    ]
+    blocks = pltpu.VMEM((16, 128, 1024), BF16)
     return pl.pallas_call(
-        middle_kernel,
-        name="middle",
+        front_kernel,
+        name="front",
         out_shape=(
-            shape((128, 1024), F32), shape((128, 1024), F32), shape((64, 2048)),
-            shape((16, 128, 1024)), shape((352, 1024)), shape((256, 1024)),
-            shape((1, 1024), F32), shape((16, 64, 1024)),
+            shape((208, 1024)), shape((128, 1024), F32), shape((128, 1024), F32),
+            shape((64, 2048)), shape((352, 1024)), shape((256, 1024)), shape((1, 1024), F32),
+            shape((16, 64, 1024)), shape((16, 128, 1024)), shape((16, 128, 1024)), *heads,
         ),
-        in_specs=[VMEM] * 7 + [ANY],
-        out_specs=(VMEM,) * 3 + (ANY,) + (VMEM,) * 4,
+        in_specs=[VMEM, VMEM, ANY] + [VMEM] * 7,
+        out_specs=(VMEM,) * 8 + (ANY,) * 9,
         scratch_shapes=[
-            pltpu.VMEM((16, 128, 1024), BF16),
-            pltpu.VMEM((16, 128, 1024), BF16),
+            blocks, blocks, blocks, blocks, blocks,
+            pltpu.VMEM((64, 2048), BF16),
+            pltpu.VMEM((64, 2048), BF16),
+            pltpu.VMEM((64, 2048), BF16),
+            pltpu.VMEM((2048, 64), BF16),
+            pltpu.VMEM((2048, 64), BF16),
+            pltpu.VMEM((2048, 64), BF16),
+            pltpu.VMEM((64, 2048), F32),
+            pltpu.VMEM((1, 2048), F32),
+            pltpu.VMEM((3, 128, 128), BF16),
+            pltpu.VMEM((176, 128), F32),
+            pltpu.VMEM((208, 128), BF16),
+            pltpu.VMEM((352, 128), BF16),
+            pltpu.VMEM((32, 1024), BF16),
+            pltpu.VMEM((64, 2048), BF16),
+            pltpu.VMEM((16, 64, 128), BF16),
+            pltpu.VMEM((16, 64, 128), BF16),
+            pltpu.VMEM((1024, 1024), BF16),
+            pltpu.VMEM((352, 1024), BF16),
+            pltpu.VMEM((256, 1024), BF16),
+            pltpu.VMEM((176, 1024), BF16),
             pltpu.VMEM((176, 2048), BF16),
             pltpu.VMEM((352, 2048), BF16),
-            pltpu.VMEM((176, 1024), BF16),
-            pltpu.VMEM((16, 128, 1024), BF16),
-            pltpu.VMEM((16, 128, 1024), BF16),
             pltpu.VMEM((128, 1024), F32),
-        ] + scatter_scratch(128, 1024) + [
-            pltpu.VMEM((16, 64, 128), BF16),
-            dma(50), dma(50), dma(2),
-        ],
-        compiler_params=params(2),
-    )(hidden, att, w_out, w_q, w_gu, down_all, grad, dy_all)
+        ] + scatter_scratch(128, 1024) + [dma(140), dma(140), dma(33)],
+        compiler_params=params(1),
+    )(hidden, grad, wqkv, wout, wgu, wdown, g1, g2, cos, sin)
 
 
 LATE = 224
@@ -681,11 +670,11 @@
     k_ref, v_ref, kt_ref, qt_ref, q_ref, dot_ref, ot_ref, lse_ref, cos_ref, sin_ref,
     n1_ref, wq_ref, h_ref, h1_ref, dh1_ref, downpart_ref, ggu_ref, gdown_ref, ggain_ref, gout_ref,
     result_ref, dinput_ref, gupieces_ref, rowpieces_ref, latepieces_ref,
-    n1, downpart, dproj, dk, dv, part, late, rows_in,
+    n1, downpart, gsum, dproj, dk, dv, part, late, rows_in,
     total, gout, gu_sum, row_sum, late_sum, *rest,
 ):
     (
-        core_a, mid_a, far_a, core_b, mid_b, far_b, core_c, mid_c, far_c,
+        core_a, far_a, core_b, far_b, core_c, far_c,
         gu_along, gu_across, gu_keep, row_along, row_across, row_keep,
         late_along, late_across, late_keep, send, recv, local,
     ) = rest
@@ -696,6 +685,7 @@
          gu_keep.at[pl.ds(0, 176)], late_keep, late_keep.at[pl.ds(0, LATE // 2)]],
     )
     loads = [
+        pltpu.make_async_copy(gout_ref, gsum, local.at[5]),
         pltpu.make_async_copy(downpart_ref, downpart, local.at[0]),
         pltpu.make_async_copy(n1_ref, n1, local.at[1]),
     ]
@@ -703,13 +693,18 @@
         copy.start()
     greet(ctx_peers(p) + p.fsdp_peers)
     loads[0].wait()
-    down = scatter_ctx(p, links, 0, downpart, total.at[0], core_a, mid_a, far_a, 128)
-    next(down)
+    sum_out = scatter_ctx(p, links, 16, gsum, gout, core_b, far_b, 64)
+    next(sum_out)
     sum_gu = scatter_fsdp(
         p, links, 48, lambda f: ggu_ref.at[:, lanes_of(f)], gu_along, gu_across, gu_keep, gu_sum, 352
     )
     next(sum_gu)
-    sum_out = scatter_ctx(p, links, 16, gout_ref, gout, core_b, mid_b, far_b, 64)
+    loads[1].wait()
+    down = scatter_ctx(p, links, 0, downpart, total.at[0], core_a, far_a, 128)
+    next(down)
+    sum_rows = scatter_fsdp(
+        p, links, 55, lambda f: rows_in.at[f], row_along, row_across, row_keep, row_sum, 32
+    )
     all_gu = gather_ctx(p, links, 69, gu_sum, gupieces_ref, 352)
     mine = [
         pltpu.make_async_copy(gu_sum, gupieces_ref.at[p.c], local.at[2]),
@@ -724,9 +719,19 @@
     def step(stages):
         return lambda: next(stages, None)
 
+    def begin_rows():
+        next(sum_out, None)
+        for f in range(8):
+            rows_in[f, pl.ds(0, 16), :] = gdown_ref[pl.ds(32 * f, 16), :]
+            tail = gdown_ref[pl.ds(32 * f + 16, 16), :].astype(F32)[:8]
+            outs = gout[pl.ds(8 * f, 8), :]
+            rows_in[f, pl.ds(16, 16), :] = jnp.concatenate([tail, outs], axis=0).astype(BF16)
+        next(sum_rows)
+
     plan = {
-        1: [step(down)], 2: [step(sum_out)], 3: [step(sum_gu)], 4: [step(down)],
-        5: [step(down), begin_gu], 6: [step(down)], 7: [step(sum_out), step(all_gu)],
+        0: [step(sum_out)], 1: [step(down)], 2: [step(sum_out)], 3: [step(sum_out)],
+        4: [step(sum_gu), step(sum_out)], 5: [step(down), begin_rows], 6: [step(down), begin_gu],
+        7: [step(down)],
     }
     dk[...] = jnp.zeros_like(dk)
     dv[...] = jnp.zeros_like(dv)
@@ -763,12 +768,14 @@
         return 0
 
     lax.fori_loop(0, 16, project, 0)
-    back = scatter_ctx(p, links, 32, part, total.at[1], core_c, mid_c, far_c, 128)
+    back = scatter_ctx(p, links, 32, part, total.at[1], core_c, far_c, 128)
     next(back)
     next(back)
     next(down, None)
     result_ref[...] = (h1_ref[...] + total[0]).astype(BF16)
-    loads[1].wait()
+    next(sum_rows)
+    next(all_gu)
+    loads[2].wait()
     gain = wq_ref[pl.ds(192, 1), :].astype(F32)
     late[...] = jnp.zeros_like(late)
     ggain = []
@@ -787,34 +794,22 @@
     )
     next(sum_late)
     next(back)
-    next(sum_out, None)
-    next(all_gu, None)
-    next(back)
-    for _ in sum_out:
-        pass
-    for f in range(8):
-        rows_in[f, pl.ds(0, 16), :] = gdown_ref[pl.ds(32 * f, 16), :]
-        tail = gdown_ref[pl.ds(32 * f + 16, 16), :].astype(F32)[:8]
-        outs = gout[pl.ds(8 * f, 8), :]
-        rows_in[f, pl.ds(16, 16), :] = jnp.concatenate([tail, outs], axis=0).astype(BF16)
-    sum_rows = scatter_fsdp(
-        p, links, 55, lambda f: rows_in.at[f], row_along, row_across, row_keep, row_sum, 32
-    )
-    next(sum_rows)
+    next(sum_rows, None)
+    all_rows = gather_ctx(p, links, 88, row_sum, rowpieces_ref, 32)
+    next(all_rows)
+    next(all_gu)
     next(back)
     next(sum_late)
-    next(all_gu, None)
+    next(back)
+    next(all_rows)
+    next(all_gu)
+    next(sum_late, None)
+    all_late = gather_ctx(p, links, 107, late_sum, latepieces_ref, LATE)
+    next(all_late)
     next(back, None)
     xhat, inv = normalize(h_ref[...].astype(F32))
     d_in = norm_back(total[1], xhat, inv, gain)
     dinput_ref[...] = (dh1_ref[...] + d_in).astype(BF16)
-    next(sum_late, None)
-    all_late = gather_ctx(p, links, 107, late_sum, latepieces_ref, LATE)
-    next(all_late)
-    next(sum_rows)
-    next(sum_rows, None)
-    all_rows = gather_ctx(p, links, 88, row_sum, rowpieces_ref, 32)
-    next(all_rows)
     for copy in mine:
         copy.start()
     run_all([all_gu, all_late, all_rows])
@@ -831,11 +826,12 @@
             shape((128, 1024)), shape((128, 1024)), shape((16, 352, 128)),
             shape((16, 32, 1024)), shape((16, LATE, 128)),
         ),
-        in_specs=[VMEM] * 10 + [ANY] + [VMEM] * 4 + [ANY] + [VMEM] * 4,
+        in_specs=[VMEM] * 10 + [ANY] + [VMEM] * 4 + [ANY] + [VMEM] * 3 + [ANY],
         out_specs=(VMEM, VMEM, ANY, ANY, ANY),
         scratch_shapes=[
             pltpu.VMEM((16, 128, 1024), BF16),
             pltpu.VMEM((16, 128, 1024), BF16),
+            pltpu.VMEM((16, 64, 1024), BF16),
             pltpu.VMEM((192, 2048), BF16),
             pltpu.VMEM((2048, 64), F32),
             pltpu.VMEM((2048, 64), F32),
@@ -849,7 +845,7 @@
             pltpu.VMEM((LATE, 128), BF16),
         ] + scatter_scratch(128, 1024) + scatter_scratch(64, 1024) + scatter_scratch(128, 1024)
         + fsdp_scratch(352, 128) + fsdp_scratch(32, 1024) + fsdp_scratch(LATE, 128)
-        + [dma(126), dma(126), dma(5)],
+        + [dma(126), dma(126), dma(6)],
         compiler_params=params(3),
     )(*args)
 
@@ -911,13 +907,11 @@
     cos, sin = rope_tables()
     cos, sin = jnp.asarray(cos), jnp.asarray(sin)
     (
-        att_t, dy_all, w_q, w_gu, w_out, down_all, n1, q_t, k_t, v_t, queries, keys, values, o_t, lse
-    ) = forward(
+        w_q, h1, d_h1, do_t, g_gu, g_down, g_gain_two, g_out,
+        n1, down_part, q_t, k_t, queries, keys, values, o_t, lse,
+    ) = front(
         hidden_b, grad_b, qkv_weight, out_weight, gate_up_weight, down_weight,
         attn_gain[None], mlp_gain[None], cos, sin,
-    )
-    h1, d_h1, do_t, down_part, g_gu, g_down, g_gain_two, g_out = middle(
-        hidden_b, att_t, w_out, w_q, w_gu, down_all, grad_b, dy_all
     )
     result, input_grad, gu_pieces, row_pieces, late_pieces = backward(
         keys, values, k_t, q_t, queries, do_t, o_t, lse, cos, sin,

time: 234 us -> 208 us (0.89)
  Pallas kernels: 220 us -> 194 us
    pallas_call x1, Pallas kernels: 87.5 us -> 73.2 us  [backward(): pl.pallas_call(backward_kernel, name='backward', out_shape=(shape((128, 1...]
    pallas_call x2 -> x1, Pallas kernels: 133 us -> 121 us  [front(): pl.pallas_call(front_kernel, name='front', out_shape=(shape((208, 1024)),...]
where the time goes in v2:
time: 208 us
  Pallas kernels  194 us (93%)
  local copies, waits for them, and re-layouts  9.6 us (5%)
  other arithmetic  3.47 us (2%)
    pallas_call x1, Pallas kernels, front(): pl.pallas_call(front_kernel, name='front', out_shape=(shape((208, 1024)),...  121 us
    pallas_call x1, Pallas kernels, backward(): pl.pallas_call(backward_kernel, name='backward', out_shape=(shape((128, 1...  73.2 us
    unnamed x13, local copies, waits for them, and re-layouts  5.86 us

profile of v2, /device:TPU:1, one launch (start us, length us, event | category | flops | bytes accessed | tf_op | source)
XLA Modules:
  0.0 207.9 jit_solution(11757504516025456421)
XLA Ops:
  0.6 120.9 %front.1 = (bf16[208,1024]{1,0:T(8,128)(2,1)}, f32[128,1024]{1,0:T(8,128)}, f32[128,1024]{1,0:T(8,128)}, bf16[64,2048]{1,0:T(8,128)(2,1)}, bf16[352,1024]{1,0:T(...) custom-call(bf16[128,1024]{1,0:T(8,128)(2,1)} %bitcast.34, ...), custom_call_target="tpu_custom_call" | custom-call | tf_op jit(solution)/shard_map/front/pallas_call | solution.py:626
  121.5 73.2 %backward.1 = (bf16[128,1024]{1,0:T(8,128)(2,1)}, bf16[128,1024]{1,0:T(8,128)(2,1)}, bf16[16,352,128]{2,1,0:T(8,128)(2,1)}, bf16[16,32,1024]{2,1,0:T(8,128)(2,1)}, bf16[16,224,128]{2,1,0:T(8,128)(2,1)}) custom-call(bf16[2048,64]{1,0:T(8,128)(2,1)} %get-tuple-element.30.k_ref, bf16[2048,64]{1,0:T(8,128)(2,1)} %get-tuple-element.31.v_ref, ...), custom_call_target="tpu_custom_call" | custom-call | tf_op jit(solution)/shard_map/backward/pallas_call | solution.py:822
  194.8 1.8 bitcast_convert_fusion
  196.6 1.2 slice_bitcast_fusion
  197.8 0.0 copy-start.1
  197.8 0.4 copy.21
  198.2 1.2 slice_convert_fusion
  199.4 0.0 copy-done.1
  199.4 0.1 slice.37
  199.5 0.4 copy.24
  199.9 0.1 slice.38
  200.0 0.3 convert_bitcast_fusion
  200.2 2.3 %copy.23 = f32[128,5248]{1,0:T(8,128)} copy(f32[128,5248]{0,1:T(8,128)S(1)} %convert_bitcast_fusion) | data formatting | bytes 5373952
  202.5 1.3 slice.36
  203.8 0.2 copy.19
  203.9 0.0 copy-start
  204.0 1.6 copy.22
  205.6 0.0 copy-done
  205.6 0.0 copy-start.3
  205.6 0.0 copy-start.2
  205.6 0.2 convert_element_type.16
  205.8 0.5 slice_bitcast_fusion.1
  206.3 0.2 copy-done.3
  206.5 0.7 copy.27
  207.2 0.0 copy-done.2
  207.2 0.7 copy.28
  (1 shorter events, 0.0 us)
Async XLA Ops:
  197.8 1.6 copy-start.1
  203.9 1.6 copy-start
  205.6 1.0 copy-start.3
  205.6 1.7 copy-start.2

commit v3 on v2

--- a/solution.py
+++ b/solution.py
@@ -45,6 +45,10 @@
 
         self.same_core = {name: chip * 2 + k for name, chip in self.chip.items()}
         self.cross_core = {name: chip * 2 + 1 - k for name, chip in self.chip.items()}
+        self.xl = xl
+        self.t = c % 8
+        self.column = {name: chip % 4 * 2 + k for name, chip in self.chip.items()}
+        self.cross_column = {name: chip % 4 * 2 + 1 - k for name, chip in self.chip.items()}
         self.ring = [(c + d) % 16 for d in range(16)]
         z, xh = self.f // 2, self.f % 2
         self.twin = z * 2 + 1 - xh
@@ -107,13 +111,18 @@
 GATHER_COPIES = 19
 
 
-def gather_ctx(p, links, base, own, out, rows):
+def gather_ctx(p, links, base, own, out, rows, off=None):
     half = rows // 2
     top, bottom = pl.ds(0, half), pl.ds(half, half)
     to_p, to_m, to_x, to_k = (
         on_ctx(p.same("P")), on_ctx(p.same("M")), on_ctx(p.same("X")), on_ctx(p.other),
     )
-    mine = out.at[p.c]
+
+    def rows_of(ref):
+        return ref if off is None else ref.at[pl.ds(off, rows)]
+
+    own = rows_of(own)
+    mine = rows_of(out.at[p.c])
 
     def put(i, src, dst, peer):
         links.put(base + i, src, dst, peer)
@@ -122,10 +131,10 @@
         links.got(base + i, dst)
 
     def block(name):
-        return out.at[p.same(name)]
+        return rows_of(out.at[p.same(name)])
 
     def cross(name):
-        return out.at[p.cross(name)]
+        return rows_of(out.at[p.cross(name)])
 
     put(0, own, mine, to_p)
     put(1, own, mine, to_m)
@@ -172,6 +181,85 @@
     yield [p.cross("XF")]
 
 
+def gather_column(p, links, base, own, out, rows):
+    half = rows // 2
+    top, bottom = pl.ds(0, half), pl.ds(half, half)
+    to_p, to_m, to_k = on_ctx(p.same("P")), on_ctx(p.same("M")), on_ctx(p.other)
+    same, cross = p.column, p.cross_column
+
+    def put(i, src, dst, peer):
+        links.put(base + i, src, dst, peer)
+
+    def got(i, dst):
+        links.got(base + i, dst)
+
+    mine = out.at[same["S"]]
+    put(0, own, mine, to_p)
+    put(1, own, mine, to_m)
+    put(2, own, mine, to_k)
+    yield [same["S"]]
+    got(0, out.at[same["M"]])
+    put(3, out.at[same["M"], top], out.at[same["M"], top], to_p)
+    put(5, out.at[same["M"]], out.at[same["M"]], to_k)
+    got(1, out.at[same["P"]])
+    put(4, out.at[same["P"], bottom], out.at[same["P"], bottom], to_m)
+    put(6, out.at[same["P"]], out.at[same["P"]], to_k)
+    got(2, out.at[cross["S"]])
+    yield [cross["S"], same["M"], same["P"]]
+    got(5, out.at[cross["M"]])
+    got(3, out.at[same["F"], top])
+    put(7, out.at[same["F"], top], out.at[same["F"], top], to_k)
+    got(4, out.at[same["F"], bottom])
+    put(8, out.at[same["F"], bottom], out.at[same["F"], bottom], to_k)
+    got(6, out.at[cross["P"]])
+    yield [same["F"], cross["M"], cross["P"]]
+    got(7, out.at[cross["F"], top])
+    got(8, out.at[cross["F"], bottom])
+    yield [cross["F"]]
+
+
+def scatter_column(p, links, base, part, total, core_in, far, rows):
+    half = rows // 2
+    whole, top, bottom = pl.ds(0, rows), pl.ds(0, half), pl.ds(half, half)
+    to_p, to_m, to_k = on_ctx(p.same("P")), on_ctx(p.same("M")), on_ctx(p.other)
+    order = ("F", "P", "M", "S")
+    mid = [part.at[p.column[name]] for name in order]
+
+    def put(i, src, dst, peer):
+        links.put(base + i, src, dst, peer)
+
+    def got(i, dst):
+        links.got(base + i, dst)
+
+    for i, name in enumerate(order):
+        put(i, part.at[p.cross_column[name]], core_in.at[i], to_k)
+    yield
+
+    def pair(i):
+        got(i, core_in.at[i])
+        return [(mid[i], 0), (core_in.at[i], 0)]
+
+    add_rows(mid[0], pair(0), rows)
+    put(4, mid[0].at[top], far.at[0, top], to_p)
+    put(5, mid[0].at[bottom], far.at[0, bottom], to_m)
+    yield
+    terms = pair(1)
+    got(4, far.at[0, top])
+    add_rows(mid[1], terms + [(far.at[0], 0)], half)
+    add_rows(mid[1], terms, half, half)
+    put(6, mid[1], far.at[1], to_p)
+    terms = pair(2)
+    got(5, far.at[0, bottom])
+    add_rows(mid[2], terms, half)
+    add_rows(mid[2], terms + [(far.at[0], 0)], half, half)
+    put(7, mid[2], far.at[2], to_m)
+    yield
+    terms = pair(3)
+    got(6, far.at[1])
+    got(7, far.at[2])
+    add_rows(total, terms + [(far.at[1], 0), (far.at[2], 0)], rows)
+
+
 def gather_fsdp(p, links, base, own, slot):
     links.put(base, own, slot(p.f), {"fsdp": p.twin})
     for d in (1, 3, 2):
@@ -189,6 +277,30 @@
     yield [p.planes[d] for d in (3, 1, 2)] + [p.twin_planes[d] for d in (3, 1, 2)]
 
 
+def gather_ring(p, links, base, own, slot):
+    up, down = {"fsdp": p.planes[1]}, {"fsdp": p.planes[3]}
+    links.put(base + 1, own, slot(p.f), up)
+    links.put(base + 2, own, slot(p.f), down)
+    links.put(base, own, slot(p.f), {"fsdp": p.twin})
+    yield []
+    links.got(base, slot(p.twin))
+    links.put(base + 4, slot(p.twin), slot(p.twin), up)
+    links.put(base + 5, slot(p.twin), slot(p.twin), down)
+    below = slot(p.planes[3])
+    links.got(base + 1, below)
+    links.put(base + 3, below, below, up)
+    yield []
+    above = slot(p.twin_planes[1])
+    links.got(base + 5, above)
+    links.put(base + 6, above, above, down)
+    yield []
+    links.got(base + 2, slot(p.planes[1]))
+    links.got(base + 3, slot(p.planes[2]))
+    links.got(base + 4, slot(p.twin_planes[3]))
+    links.got(base + 6, slot(p.twin_planes[2]))
+    yield []
+
+
 def scatter_fsdp(p, links, base, part, along, across, keep, total, rows):
     for n, d in enumerate((1, 3, 2)):
         links.put(base + n, part(p.planes[d]), along.at[n], {"fsdp": p.planes[d]})
@@ -226,18 +338,32 @@
     step = 16
 
     def one(i, _):
-        r = pl.multiple_of(i * step, step)
+        r = pl.ds(pl.multiple_of(i * step, step) + at, step)
         total = None
-        for ref, off in terms:
-            part = ref[pl.ds(r + off, step), :].astype(F32)
+        for ref, _unused in terms:
+            part = ref[r, :].astype(F32)
             total = part if total is None else total + part
-        dst[pl.ds(r + at, step), :] = total.astype(dst.dtype)
+        dst[r, :] = total.astype(dst.dtype)
         return 0
 
     lax.fori_loop(0, rows // step, one, 0)
 
 
-def scatter_ctx(p, links, base, part, total, core_in, far, rows):
+def lockstep(*stages):
+    while True:
+        found = []
+        ended = 0
+        for one in stages:
+            try:
+                found += next(one) or []
+            except StopIteration:
+                ended += 1
+        if ended == len(stages):
+            return
+        yield found
+
+
+def scatter_ctx(p, links, base, part, total, core_in, far, rows, off=0):
     half = rows // 2
     to_p, to_m, to_x, to_k = (
         on_ctx(p.same("P")), on_ctx(p.same("M")), on_ctx(p.same("X")), on_ctx(p.other),
@@ -249,47 +375,49 @@
     def got(i, dst):
         links.got(base + i, dst)
 
+    whole = pl.ds(off, rows)
+    top, bottom = pl.ds(off, half), pl.ds(off + half, half)
     mid = [part.at[p.same(name)] for name in SCATTER_ORDER]
     for i, name in enumerate(SCATTER_ORDER):
-        put(i, part.at[p.cross(name)], core_in.at[i], to_k)
+        put(i, part.at[p.cross(name), whole], core_in.at[i, whole], to_k)
     yield
 
     def pair(i):
-        got(i, core_in.at[i])
+        got(i, core_in.at[i, whole])
         return [(mid[i], 0), (core_in.at[i], 0)]
 
     for i, peer in ((0, to_x), (1, to_p), (2, to_m)):
-        add_rows(mid[i], pair(i), rows)
-        put(8 + i, mid[i], far.at[i], peer)
+        add_rows(mid[i], pair(i), rows, off)
+        put(8 + i, mid[i].at[whole], far.at[i, whole], peer)
     yield
     terms = pair(3)
-    got(8, far.at[0])
-    add_rows(mid[3], terms + [(far.at[0], 0)], rows)
-    put(11, mid[3].at[pl.ds(0, half)], far.at[3, pl.ds(0, half)], to_p)
-    put(12, mid[3].at[pl.ds(half, half)], far.at[3, pl.ds(half, half)], to_m)
+    got(8, far.at[0, whole])
+    add_rows(mid[3], terms + [(far.at[0], 0)], rows, off)
+    put(11, mid[3].at[top], far.at[3, top], to_p)
+    put(12, mid[3].at[bottom], far.at[3, bottom], to_m)
     yield
     terms = pair(4)
-    got(9, far.at[1])
-    got(10, far.at[2])
-    add_rows(mid[4], terms + [(far.at[1], 0), (far.at[2], 0)], rows)
-    put(13, mid[4], far.at[4], to_x)
+    got(9, far.at[1, whole])
+    got(10, far.at[2, whole])
+    add_rows(mid[4], terms + [(far.at[1], 0), (far.at[2], 0)], rows, off)
+    put(13, mid[4].at[whole], far.at[4, whole], to_x)
     yield
     terms = pair(5)
-    got(11, far.at[3, pl.ds(0, half)])
-    add_rows(mid[5], terms + [(far.at[3], 0)], half)
-    add_rows(mid[5], [(r, half) for r, _ in terms], half, half)
-    put(14, mid[5], far.at[5], to_p)
+    got(11, far.at[3, top])
+    add_rows(mid[5], terms + [(far.at[3], 0)], half, off)
+    add_rows(mid[5], terms, half, off + half)
+    put(14, mid[5].at[whole], far.at[5, whole], to_p)
     terms = pair(6)
-    got(12, far.at[3, pl.ds(half, half)])
-    add_rows(mid[6], terms, half)
-    add_rows(mid[6], [(r, half) for r, _ in terms] + [(far.at[3], half)], half, half)
-    put(15, mid[6], far.at[6], to_m)
+    got(12, far.at[3, bottom])
+    add_rows(mid[6], terms, half, off)
+    add_rows(mid[6], terms + [(far.at[3], 0)], half, off + half)
+    put(15, mid[6].at[whole], far.at[6, whole], to_m)
     yield
     terms = pair(7)
-    got(13, far.at[4])
-    got(14, far.at[5])
-    got(15, far.at[6])
-    add_rows(total, terms + [(far.at[4], 0), (far.at[5], 0), (far.at[6], 0)], rows)
+    got(13, far.at[4, whole])
+    got(14, far.at[5, whole])
+    got(15, far.at[6, whole])
+    add_rows(total, terms + [(far.at[4], 0), (far.at[5], 0), (far.at[6], 0)], rows, off)
 
 
 def scatter_scratch(rows, cols):
@@ -299,6 +427,10 @@
     ]
 
 
+def column_scratch(rows, cols):
+    return [pltpu.VMEM((4, rows, cols), BF16), pltpu.VMEM((3, rows, cols), BF16)]
+
+
 def dma(n):
     return pltpu.SemaphoreType.DMA((n,))
 
@@ -310,6 +442,7 @@
 
 
 Q_BLOCK = 256
+UNITS = 352
 
 
 def pick_rows(select, matrix):
@@ -322,11 +455,8 @@
     return jnp.where((col == row + shift) & (row < valid), 1.0, 0.0)
 
 
-def unit_of(row, c):
-    shard = sum(((row >= 21 * n).astype(jnp.int32) for n in range(1, 8)), 0)
-    place = row - 21 * shard
-    inside = (row < 168) & ((place < 20) | (c < 8))
-    return jnp.where(inside, 328 * shard + 16 * place + c, -1)
+def shard_of(row):
+    return sum(((row >= 41 * n).astype(jnp.int32) for n in range(1, 8)), 0)
 
 
 def iota(dims, axis):
@@ -335,11 +465,12 @@
 
 def front_kernel(
     h_ref, dy_ref, wqkv_ref, wout_ref, wgu_ref, wdown_ref, g1_ref, g2_ref, cos_ref, sin_ref,
-    wq_ref, h1_ref, dh1_ref, dot_ref, ggu_ref, gdown_ref, ggain_ref, gout_ref,
-    n1_ref, downpart_ref, qt_out, kt_out, qr_out, kr_out, vr_out, ot_out, lse_out,
-    hall, n1, dyall, nall, part, qt_ref, kt_ref, vt_ref, qr_ref, kr_ref, vr_ref, ot_ref, lse_ref,
+    wq_ref, result_ref, dh1_ref, dot_ref, gusum_ref, gdown_ref, ggain_ref, gout_ref,
+    n1_ref, qt_out, kt_out, qr_out, kr_out, vr_out, ot_out, lse_out,
+    hall, n1, dyall, nall, part, downsum, qt_ref, kt_ref, vt_ref, qr_ref, kr_ref, vr_ref, ot_ref, lse_ref,
     qkv_win, gu_acc, qkv_cols, gu_cols, down_rows, ob, att_ref, dat,
-    woutall, gu_ref, downall, down_w, act, dgu, total, core_in, far, send, recv, local,
+    woutall, gu_ref, downall, down_w, act, dgu, total, core_in, far, ggu, gu_along, gu_across, gu_keep,
+    h1_ref, down_total, core_down, far_down, send, recv, local,
 ):
     p = Place()
     links = Links(
@@ -373,36 +504,44 @@
     gather_h = gather_ctx(p, links, 0, h_ref, hall, 128)
     ready = next(gather_h)
     lanes = lanes_of(p.f)
+    half = pl.ds(pl.multiple_of(p.k * 64, 64), 64)
+
+    def out_half(f, k):
+        return woutall.at[pl.ds(pl.multiple_of(f * 128 + k * 64, 64), 64)]
+
+    gather_out = gather_ring(p, links, 53, wout_ref.at[half], lambda f: out_half(f, p.k))
+    next(gather_out)
     wq_ref[:, lanes] = qkv_cols[...]
     for half in range(2):
-        want = unit_of(iota((176, 1), 0), p.c)
-        want = jnp.where(want < 0, -1, want + 64 * half)
+        row = iota((UNITS, 1), 0)
+        want = jnp.where(row < 328, 8 * row + p.t + 64 * half, -1)
         gu_acc[...] = jnp.zeros_like(gu_acc)
 
         def pick(i, _):
             cols = pl.ds(pl.multiple_of(2560 * half + i * 896, 128), 896)
-            select = jnp.where(iota((176, 896), 1) + i * 896 == want, 1.0, 0.0)
+            select = jnp.where(iota((UNITS, 896), 1) + i * 896 == want, 1.0, 0.0)
             gu_acc[...] += nt(select.astype(BF16), wgu_ref[:, cols])
             return 0
 
         lax.fori_loop(0, 3, pick, 0)
-        gu_cols[pl.ds(176 * half, 176), :] = gu_acc[...].astype(BF16)
-    place = iota((32, 328), 0)
-    select = (iota((32, 328), 1) == 16 * place + p.c) & (place < 21)
+        gu_cols[pl.ds(UNITS * half, UNITS), :] = gu_acc[...].astype(BF16)
+    place = iota((48, 328), 0)
+    select = (iota((48, 328), 1) == 8 * place + p.t) & (place < 41)
     down_rows[...] = nn(jnp.where(select, 1.0, 0.0).astype(BF16), wdown_ref[...]).astype(BF16)
+    gather_gu = gather_ring(p, links, 45, gu_cols, lambda f: gu_ref.at[:, lanes_of(f)])
+    next(gather_gu)
+
+    def down_slot(f):
+        return downall.at[pl.ds(pl.multiple_of(f * 48, 16), 48)]
+
+    gather_down = gather_ring(p, links, 83, down_rows, down_slot)
+    next(gather_down)
     own_h.wait()
     next(gather_wq)
     ready += next(gather_h)
     next(gather_wq)
-    gather_gu = gather_fsdp(p, links, 45, gu_cols, lambda f: gu_ref.at[:, lanes_of(f)])
-    next(gather_gu)
-    def down_slot(f):
-        return downall.at[pl.ds(pl.multiple_of(f * 32, 32), 32)]
-
-    gather_down = gather_fsdp(p, links, 83, down_rows, down_slot)
-    next(gather_down)
     locals_ = [
-        pltpu.make_async_copy(dy_ref, dyall.at[p.c], local.at[6]),
+        pltpu.make_async_copy(dy_ref, dyall.at[p.t], local.at[6]),
         pltpu.make_async_copy(
             wout_ref, woutall.at[pl.ds(pl.multiple_of(p.f * 128, 128), 128)], local.at[8]
         ),
@@ -411,12 +550,6 @@
     for copy in locals_:
         copy.start()
     gu_ref[:, lanes] = gu_cols[...]
-    half = pl.ds(pl.multiple_of(p.k * 64, 64), 64)
-
-    def out_half(f, k):
-        return woutall.at[pl.ds(pl.multiple_of(f * 128 + k * 64, 64), 64)]
-
-    gather_out = gather_fsdp(p, links, 53, wout_ref.at[half], lambda f: out_half(f, p.k))
     next(gather_out)
     saves = []
 
@@ -451,7 +584,7 @@
     for b in next(gather_h):
         project(b)
     ready = next(gather_h)
-    gather_dy = gather_ctx(p, links, 19, dy_ref, dyall, 128)
+    gather_dy = gather_column(p, links, 19, dy_ref, dyall, 128)
     next(gather_dy)
     for b in ready:
         project(b)
@@ -459,10 +592,10 @@
         ready = next(gather_h, None)
         for b in ready or ():
             project(b)
+    next(gather_out)
     next(gather_gu)
     next(gather_down)
-    twins = next(gather_out)
-    plan = {1: gather_dy, 3: gather_dy, 4: gather_out, 6: gather_dy}
+    plan = {1: gather_dy, 2: gather_gu, 3: gather_down, 4: gather_out, 5: gather_dy}
 
     def attend(i, _):
         j = (p.c // 2 + i) % 8
@@ -510,7 +643,7 @@
     ]
     for copy in saves[16:]:
         copy.start()
-    others = twins + [p.planes[d] for d in (3, 1, 2)] + [p.twin_planes[d] for d in (3, 1, 2)]
+    others = [p.twin] + [p.planes[d] for d in (3, 1, 2)] + [p.twin_planes[d] for d in (3, 1, 2)]
     for i, f in enumerate(others):
         links.put(60 + i, out_half(f, p.k), out_half(f, p.k), on_ctx(p.other))
     for d in range(1, 16):
@@ -526,70 +659,75 @@
     h1 = h_ref[...].astype(F32) + tn(att, woutall[...])
     h1_ref[...] = h1
     xhat, _unused = normalize(h1)
-    nall[p.c] = (xhat * gain).astype(BF16)
-    gather = gather_ctx(p, links, 90, nall.at[p.c], nall, 128)
+    nall[p.t] = (xhat * gain).astype(BF16)
+    gather = gather_column(p, links, 90, nall.at[p.t], nall, 128)
     ready = next(gather)
     next(gather_gu)
     next(gather_down)
-    pick = iota((176, 256), 1)
-    row = iota((176, 1), 0)
-    shard = sum(((row >= 21 * n).astype(jnp.int32) for n in range(1, 8)), 0)
-    want = jnp.where(row < 168, row + 11 * shard, -1)
+    pick = iota((UNITS, 384), 1)
+    row = iota((UNITS, 1), 0)
+    want = jnp.where(row < 328, row + 7 * shard_of(row), -1)
     down_w[...] = nn(jnp.where(pick == want, 1.0, 0.0).astype(BF16), downall[...]).astype(BF16)
     for _ in gather_dy:
         pass
 
-    def feed(b):
-        n2 = nall[b]
+    def feed(b, other):
+        n2 = jnp.concatenate([nall[b], nall[other]], axis=0)
         gu = nt(gu_ref[...], n2)
-        d_act = nt(down_w[...], dyall[b])
-        gate, up = gu[:176], gu[176:]
+        d_act = nt(down_w[...], jnp.concatenate([dyall[b], dyall[other]], axis=0))
+        gate, up = gu[:UNITS], gu[UNITS:]
         cdf = 0.5 * (1.0 + lax.erf(gate * 2.0 ** (-0.5)))
         gelu = gate * cdf
         pdf = jnp.exp(-0.5 * gate * gate) * (2.0 * np.pi) ** (-0.5)
         d_gate = d_act * up * (cdf + gate * pdf)
         d_gu = jnp.concatenate([d_gate, d_act * gelu], axis=0).astype(BF16)
-        at = pl.ds(pl.multiple_of(b * 128, 128), 128)
-        act[:, at] = (gelu * up).astype(BF16)
-        dgu[:, at] = d_gu
-        part[b] = tn(d_gu, gu_ref[...]).astype(BF16)
-
-    while ready is not None:
-        for b in ready:
-            feed(b)
-        ready = next(gather, None)
-    scatter = scatter_ctx(p, links, 109, part, total, core_in, far, 128)
+        activated = (gelu * up).astype(BF16)
+        d_n2 = tn(d_gu, gu_ref[...]).astype(BF16)
+        for i, block in enumerate((b, other)):
+            at = pl.ds(pl.multiple_of(block * 128, 128), 128)
+            act[:, at] = activated[:, 128 * i : 128 * i + 128]
+            dgu[:, at] = d_gu[:, 128 * i : 128 * i + 128]
+            part[block] = d_n2[128 * i : 128 * i + 128]
+
+    waiting = list(ready)
+    for found in gather:
+        waiting += found
+        while len(waiting) > 1:
+            feed(waiting.pop(0), waiting.pop(0))
+    scatter = scatter_column(p, links, 109, part, total, core_in, far, 128)
     next(scatter)
     next(scatter)
     ggain = []
     for half in range(2):
         cols = pl.ds(512 * half, 512)
-        g = nn(dgu[...], nall[:, :, cols].reshape(2048, 512))
-        ggu_ref[:, cols] = g.astype(BF16)
+        g = nn(dgu[...], nall[:, :, cols].reshape(1024, 512))
+        ggu[:, cols] = g.astype(BF16)
         ggain.append(jnp.sum(g * gu_ref[:, cols].astype(F32), axis=0, keepdims=True))
     ggain_ref[...] = jnp.concatenate(ggain, axis=1) / gain
+    sum_gu = scatter_fsdp(
+        p, links, 140, lambda f: ggu.at[:, lanes_of(f)], gu_along, gu_across, gu_keep,
+        gusum_ref, 2 * UNITS,
+    )
+    next(sum_gu)
     next(scatter)
-    row = iota((256, 1), 0)
-    shard = row // 32
-    place = row - 32 * shard
-    want = jnp.where(place < 21, 21 * shard + place, -1)
-    spread = jnp.where(iota((256, 176), 1) == want, 1.0, 0.0).astype(BF16)
+    row = iota((384, 1), 0)
+    shard = row // 48
+    place = row - 48 * shard
+    want = jnp.where(place < 41, 41 * shard + place, -1)
+    spread = jnp.where(iota((384, UNITS), 1) == want, 1.0, 0.0).astype(BF16)
     for half in range(2):
         cols = pl.ds(512 * half, 512)
-        g = nn(act[...], dyall[:, :, cols].reshape(2048, 512)).astype(BF16)
+        g = nn(act[...], dyall[:, :, cols].reshape(1024, 512)).astype(BF16)
         gdown_ref[:, cols] = nn(spread, g).astype(BF16)
-    next(scatter)
 
     def down(b, _):
         at = pl.ds(pl.multiple_of(b * 128, 128), 128)
-        hall[b] = tn(act[:, at], down_w[...]).astype(BF16)
+        downsum[b] = tn(act[:, at], down_w[...]).astype(BF16)
         return 0
 
-    next(scatter)
-    links.close(90)
-    lax.fori_loop(0, 16, down, 0)
-    store = pltpu.make_async_copy(hall, downpart_ref, local.at[4])
-    store.start()
+    lax.fori_loop(0, 8, down, 0)
+    sum_down = scatter_column(p, links, 147, downsum, down_total, core_down, far_down, 128)
+    next(sum_down)
     next(scatter, None)
     h1 = h1_ref[...]
     xhat, inv = normalize(h1)
@@ -601,14 +739,20 @@
     for d in range(1, 16):
         links.put(124 + d, dat.at[p.ring[d]], dot_ref.at[:, lanes], on_ctx(p.ring[d]))
     dot_ref[:, lanes] = dat[p.c]
+    next(sum_down)
     att = att_ref[...]
     for g in range(4):
         rows = att[4 * g : 4 * g + 4].reshape(256, 128)
         block = nn(rows, d_h1_b).reshape(2, 16, 8, 1024).transpose(1, 0, 2, 3)
         gout_ref[:, pl.ds(16 * g, 16), :] = block.reshape(16, 16, 1024).astype(BF16)
+    next(sum_down)
+    next(sum_gu)
     for d in range(1, 16):
         links.got(124 + d, dot_ref.at[:, pl.ds(pl.multiple_of(p.ring[16 - d] * 128, 128), 128)])
-    for copy in saves + [store]:
+    next(sum_down, None)
+    result_ref[...] = (h1_ref[...] + down_total[...]).astype(BF16)
+    next(sum_gu, None)
+    for copy in saves:
         copy.wait()
     links.close()
 
@@ -623,18 +767,19 @@
         shape((2048, 64)), shape((64, 2048), F32), shape((1, 2048), F32),
     ]
     blocks = pltpu.VMEM((16, 128, 1024), BF16)
+    column = pltpu.VMEM((8, 128, 1024), BF16)
     return pl.pallas_call(
         front_kernel,
         name="front",
         out_shape=(
-            shape((208, 1024)), shape((128, 1024), F32), shape((128, 1024), F32),
-            shape((64, 2048)), shape((352, 1024)), shape((256, 1024)), shape((1, 1024), F32),
-            shape((16, 64, 1024)), shape((16, 128, 1024)), shape((16, 128, 1024)), *heads,
+            shape((208, 1024)), shape((128, 1024)), shape((128, 1024), F32),
+            shape((64, 2048)), shape((2 * UNITS, 128)), shape((384, 1024)),
+            shape((1, 1024), F32), shape((16, 64, 1024)), shape((16, 128, 1024)), *heads,
         ),
         in_specs=[VMEM, VMEM, ANY] + [VMEM] * 7,
-        out_specs=(VMEM,) * 8 + (ANY,) * 9,
+        out_specs=(VMEM,) * 8 + (ANY,) * 8,
         scratch_shapes=[
-            blocks, blocks, blocks, blocks, blocks,
+            blocks, blocks, column, column, column, column,
             pltpu.VMEM((64, 2048), BF16),
             pltpu.VMEM((64, 2048), BF16),
             pltpu.VMEM((64, 2048), BF16),
@@ -644,49 +789,51 @@
             pltpu.VMEM((64, 2048), F32),
             pltpu.VMEM((1, 2048), F32),
             pltpu.VMEM((3, 128, 128), BF16),
-            pltpu.VMEM((176, 128), F32),
+            pltpu.VMEM((UNITS, 128), F32),
             pltpu.VMEM((208, 128), BF16),
-            pltpu.VMEM((352, 128), BF16),
-            pltpu.VMEM((32, 1024), BF16),
+            pltpu.VMEM((2 * UNITS, 128), BF16),
+            pltpu.VMEM((48, 1024), BF16),
             pltpu.VMEM((64, 2048), BF16),
             pltpu.VMEM((16, 64, 128), BF16),
             pltpu.VMEM((16, 64, 128), BF16),
             pltpu.VMEM((1024, 1024), BF16),
-            pltpu.VMEM((352, 1024), BF16),
-            pltpu.VMEM((256, 1024), BF16),
-            pltpu.VMEM((176, 1024), BF16),
-            pltpu.VMEM((176, 2048), BF16),
-            pltpu.VMEM((352, 2048), BF16),
+            pltpu.VMEM((2 * UNITS, 1024), BF16),
+            pltpu.VMEM((384, 1024), BF16),
+            pltpu.VMEM((UNITS, 1024), BF16),
+            pltpu.VMEM((UNITS, 1024), BF16),
+            pltpu.VMEM((2 * UNITS, 1024), BF16),
             pltpu.VMEM((128, 1024), F32),
-        ] + scatter_scratch(128, 1024) + [dma(140), dma(140), dma(33)],
+        ] + column_scratch(128, 1024) + [pltpu.VMEM((2 * UNITS, 1024), BF16)]
+        + fsdp_scratch(2 * UNITS, 128)
+        + [pltpu.VMEM((128, 1024), F32), pltpu.VMEM((128, 1024), F32)]
+        + column_scratch(128, 1024) + [dma(155), dma(155), dma(33)],
         compiler_params=params(1),
     )(hidden, grad, wqkv, wout, wgu, wdown, g1, g2, cos, sin)
 
 
-LATE = 224
+LATE = 288
 
 
 def backward_kernel(
     k_ref, v_ref, kt_ref, qt_ref, q_ref, dot_ref, ot_ref, lse_ref, cos_ref, sin_ref,
-    n1_ref, wq_ref, h_ref, h1_ref, dh1_ref, downpart_ref, ggu_ref, gdown_ref, ggain_ref, gout_ref,
-    result_ref, dinput_ref, gupieces_ref, rowpieces_ref, latepieces_ref,
-    n1, downpart, gsum, dproj, dk, dv, part, late, rows_in,
-    total, gout, gu_sum, row_sum, late_sum, *rest,
+    n1_ref, wq_ref, h_ref, dh1_ref, gu_sum, gdown_ref, ggain_ref, gout_ref,
+    dinput_ref, gupieces_ref, rowpieces_ref, latepieces_ref,
+    n1, gsum, dproj, dk, dv, part, late, gu_pair, gu_mine, row_pair, row_mine,
+    total, gout, row_sum, late_sum, *rest,
 ):
     (
-        core_a, far_a, core_b, far_b, core_c, far_c,
-        gu_along, gu_across, gu_keep, row_along, row_across, row_keep,
+        core_b, far_b, core_c, far_c,
+        row_along, row_across, row_keep,
         late_along, late_across, late_keep, send, recv, local,
     ) = rest
     p = Place()
     links = Links(
         send, recv, on_ctx(p.other),
-        [part.at[0], part.at[0, pl.ds(0, 64)], part.at[0, pl.ds(0, 32)], gu_keep,
-         gu_keep.at[pl.ds(0, 176)], late_keep, late_keep.at[pl.ds(0, LATE // 2)]],
+        [part.at[0], part.at[0, pl.ds(0, 64)], part.at[0, pl.ds(0, 32)], row_keep,
+         gu_mine, gu_mine.at[pl.ds(0, 176)], row_mine, row_mine.at[pl.ds(0, 48)], late_keep, late_keep.at[pl.ds(0, LATE // 2)]],
     )
     loads = [
         pltpu.make_async_copy(gout_ref, gsum, local.at[5]),
-        pltpu.make_async_copy(downpart_ref, downpart, local.at[0]),
         pltpu.make_async_copy(n1_ref, n1, local.at[1]),
     ]
     for copy in loads:
@@ -695,43 +842,40 @@
     loads[0].wait()
     sum_out = scatter_ctx(p, links, 16, gsum, gout, core_b, far_b, 64)
     next(sum_out)
-    sum_gu = scatter_fsdp(
-        p, links, 48, lambda f: ggu_ref.at[:, lanes_of(f)], gu_along, gu_across, gu_keep, gu_sum, 352
-    )
-    next(sum_gu)
-    loads[1].wait()
-    down = scatter_ctx(p, links, 0, downpart, total.at[0], core_a, far_a, 128)
-    next(down)
     sum_rows = scatter_fsdp(
-        p, links, 55, lambda f: rows_in.at[f], row_along, row_across, row_keep, row_sum, 32
-    )
-    all_gu = gather_ctx(p, links, 69, gu_sum, gupieces_ref, 352)
+        p, links, 55, lambda f: gdown_ref.at[pl.ds(pl.multiple_of(f * 48, 16), 48)],
+        row_along, row_across, row_keep, row_sum, 48,
+    )
+    next(sum_rows)
+    all_gu = gather_ctx(p, links, 69, gu_mine, gupieces_ref, UNITS)
     mine = [
-        pltpu.make_async_copy(gu_sum, gupieces_ref.at[p.c], local.at[2]),
-        pltpu.make_async_copy(row_sum, rowpieces_ref.at[p.c], local.at[3]),
+        pltpu.make_async_copy(gu_mine, gupieces_ref.at[p.c], local.at[2]),
+        pltpu.make_async_copy(row_mine, rowpieces_ref.at[p.c], local.at[3]),
         pltpu.make_async_copy(late_sum, latepieces_ref.at[p.c], local.at[4]),
     ]
 
+    other_half = pl.ds(pl.multiple_of(UNITS * (1 - p.xl), 16), UNITS)
+    own_half = pl.ds(pl.multiple_of(UNITS * p.xl, 16), UNITS)
+    other_cols = pl.ds(pl.multiple_of(512 * (1 - p.xl), 128), 512)
+    to_x = on_ctx(p.same("X"))
+
+    links.put(142, gu_sum.at[other_half], gu_pair, to_x)
+
     def begin_gu():
-        next(sum_gu, None)
+        links.got(142, gu_pair)
+        add_rows(gu_mine, [(gu_sum.at[own_half], 0), (gu_pair, 0)], UNITS)
         next(all_gu)
+
+    def swap_rows():
+        next(sum_rows, None)
+        links.put(143, row_sum.at[:, other_cols], row_pair, to_x)
 
     def step(stages):
         return lambda: next(stages, None)
 
-    def begin_rows():
-        next(sum_out, None)
-        for f in range(8):
-            rows_in[f, pl.ds(0, 16), :] = gdown_ref[pl.ds(32 * f, 16), :]
-            tail = gdown_ref[pl.ds(32 * f + 16, 16), :].astype(F32)[:8]
-            outs = gout[pl.ds(8 * f, 8), :]
-            rows_in[f, pl.ds(16, 16), :] = jnp.concatenate([tail, outs], axis=0).astype(BF16)
-        next(sum_rows)
-
     plan = {
-        0: [step(sum_out)], 1: [step(down)], 2: [step(sum_out)], 3: [step(sum_out)],
-        4: [step(sum_gu), step(sum_out)], 5: [step(down), begin_rows], 6: [step(down), begin_gu],
-        7: [step(down)],
+        0: [step(sum_out)], 1: [begin_gu], 3: [step(sum_out)], 4: [step(sum_out), step(sum_rows)],
+        5: [step(sum_out), step(all_gu)], 6: [step(sum_out), swap_rows], 7: [step(all_gu)],
     }
     dk[...] = jnp.zeros_like(dk)
     dv[...] = jnp.zeros_like(dv)
@@ -768,14 +912,23 @@
         return 0
 
     lax.fori_loop(0, 16, project, 0)
-    back = scatter_ctx(p, links, 32, part, total.at[1], core_c, far_c, 128)
+    back = lockstep(
+        scatter_ctx(p, links, 32, part, total, core_c, far_c, 64, 0),
+        scatter_ctx(p, links, 126, part, total, core_c, far_c, 64, 64),
+    )
     next(back)
     next(back)
-    next(down, None)
-    result_ref[...] = (h1_ref[...] + total[0]).astype(BF16)
-    next(sum_rows)
     next(all_gu)
-    loads[2].wait()
+    links.got(143, row_pair)
+    for half in range(2):
+        own_lanes = pl.ds(pl.multiple_of(512 * p.xl + 256 * half, 128), 256)
+        add_rows(
+            row_mine.at[pl.ds(48 * half, 48)],
+            [(row_sum.at[:, own_lanes], 0), (row_pair.at[:, pl.ds(256 * half, 256)], 0)], 48,
+        )
+    all_rows = gather_ctx(p, links, 88, row_mine, rowpieces_ref, 96)
+    next(all_rows)
+    loads[1].wait()
     gain = wq_ref[pl.ds(192, 1), :].astype(F32)
     late[...] = jnp.zeros_like(late)
     ggain = []
@@ -788,27 +941,31 @@
     row = iota((16, 1024), 0)
     gains = jnp.where(row == 0, gain_row, 0.0)
     late[pl.ds(192, 16), :] = jnp.where(row == 1, ggain_ref[...], gains).astype(BF16)
+    for f in range(8):
+        for g in range(4):
+            pair = gout[pl.ds(8 * f, 8), pl.ds(256 * g, 256)]
+            late[pl.ds(208 + 16 * g, 16), pl.ds(128 * f, 128)] = jnp.concatenate(
+                [pair[:, :128], pair[:, 128:]], axis=0
+            ).astype(BF16)
     sum_late = scatter_fsdp(
         p, links, 62, lambda f: late.at[:, lanes_of(f)],
         late_along, late_across, late_keep, late_sum, LATE,
     )
     next(sum_late)
     next(back)
-    next(sum_rows, None)
-    all_rows = gather_ctx(p, links, 88, row_sum, rowpieces_ref, 32)
+    next(all_gu)
     next(all_rows)
-    next(all_gu)
     next(back)
     next(sum_late)
     next(back)
+    next(all_gu)
     next(all_rows)
-    next(all_gu)
     next(sum_late, None)
     all_late = gather_ctx(p, links, 107, late_sum, latepieces_ref, LATE)
     next(all_late)
     next(back, None)
     xhat, inv = normalize(h_ref[...].astype(F32))
-    d_in = norm_back(total[1], xhat, inv, gain)
+    d_in = norm_back(total[...], xhat, inv, gain)
     dinput_ref[...] = (dh1_ref[...] + d_in).astype(BF16)
     for copy in mine:
         copy.start()
@@ -823,13 +980,12 @@
         backward_kernel,
         name="backward",
         out_shape=(
-            shape((128, 1024)), shape((128, 1024)), shape((16, 352, 128)),
-            shape((16, 32, 1024)), shape((16, LATE, 128)),
+            shape((128, 1024)), shape((16, UNITS, 128)),
+            shape((16, 96, 256)), shape((16, LATE, 128)),
         ),
-        in_specs=[VMEM] * 10 + [ANY] + [VMEM] * 4 + [ANY] + [VMEM] * 3 + [ANY],
-        out_specs=(VMEM, VMEM, ANY, ANY, ANY),
+        in_specs=[VMEM] * 10 + [ANY] + [VMEM] * 6 + [ANY],
+        out_specs=(VMEM, ANY, ANY, ANY),
         scratch_shapes=[
-            pltpu.VMEM((16, 128, 1024), BF16),
             pltpu.VMEM((16, 128, 1024), BF16),
             pltpu.VMEM((16, 64, 1024), BF16),
             pltpu.VMEM((192, 2048), BF16),
@@ -837,15 +993,17 @@
             pltpu.VMEM((2048, 64), F32),
             pltpu.VMEM((16, 128, 1024), BF16),
             pltpu.VMEM((LATE, 1024), BF16),
-            pltpu.VMEM((8, 32, 1024), BF16),
-            pltpu.VMEM((2, 128, 1024), F32),
+            pltpu.VMEM((UNITS, 128), BF16),
+            pltpu.VMEM((UNITS, 128), BF16),
+            pltpu.VMEM((48, 512), BF16),
+            pltpu.VMEM((96, 256), BF16),
+            pltpu.VMEM((128, 1024), F32),
             pltpu.VMEM((64, 1024), F32),
-            pltpu.VMEM((352, 128), BF16),
-            pltpu.VMEM((32, 1024), BF16),
+            pltpu.VMEM((48, 1024), BF16),
             pltpu.VMEM((LATE, 128), BF16),
-        ] + scatter_scratch(128, 1024) + scatter_scratch(64, 1024) + scatter_scratch(128, 1024)
-        + fsdp_scratch(352, 128) + fsdp_scratch(32, 1024) + fsdp_scratch(LATE, 128)
-        + [dma(126), dma(126), dma(6)],
+        ] + scatter_scratch(64, 1024) + scatter_scratch(128, 1024)
+        + fsdp_scratch(48, 1024) + fsdp_scratch(LATE, 128)
+        + [dma(144), dma(144), dma(6)],
         compiler_params=params(3),
     )(*args)
 
@@ -907,28 +1065,27 @@
     cos, sin = rope_tables()
     cos, sin = jnp.asarray(cos), jnp.asarray(sin)
     (
-        w_q, h1, d_h1, do_t, g_gu, g_down, g_gain_two, g_out,
-        n1, down_part, q_t, k_t, queries, keys, values, o_t, lse,
+        w_q, result, d_h1, do_t, gu_sum, g_down, g_gain_two, g_out,
+        n1, q_t, k_t, queries, keys, values, o_t, lse,
     ) = front(
         hidden_b, grad_b, qkv_weight, out_weight, gate_up_weight, down_weight,
         attn_gain[None], mlp_gain[None], cos, sin,
     )
-    result, input_grad, gu_pieces, row_pieces, late_pieces = backward(
+    input_grad, gu_pieces, row_pieces, late_pieces = backward(
         keys, values, k_t, q_t, queries, do_t, o_t, lse, cos, sin,
-        n1, w_q, hidden_b, h1, d_h1, down_part, g_gu, g_down, g_gain_two, g_out,
+        n1, w_q, hidden_b, d_h1, gu_sum, g_down, g_gain_two, g_out,
     )
     late_pieces = late_pieces.astype(F32)
     qkv_grad = (
         late_pieces[:, :192].reshape(16, 3, 64, 128).transpose(3, 1, 0, 2).reshape(128, 3072)
     )
     gain_grads = jnp.sum(late_pieces[:, 192:194], axis=0)
-    gate_up = gu_pieces.reshape(16, 2, 176, 128)[:, :, :168].transpose(1, 2, 0, 3)
-    gate_up = gate_up.reshape(2, 8, 336, 128)[:, :, :328].reshape(5248, 128)
-    gate_up_grad = gate_up.astype(F32).T
-    down_grad = (
-        row_pieces[:, :21].transpose(1, 0, 2).reshape(336, 1024)[:328].astype(F32)
-    )
-    out_weight_grad = row_pieces[:, 24:].reshape(128, 1024).astype(F32)
+    gate_up = gu_pieces.reshape(2, 8, UNITS, 128)[:, :, :328].transpose(0, 2, 1, 3)
+    gate_up_grad = gate_up.reshape(5248, 128).astype(F32).T
+    down_rows = row_pieces.reshape(2, 8, 2, 48, 256)[:, :, :, :41].transpose(3, 1, 0, 2, 4)
+    down_grad = down_rows.reshape(328, 1024).astype(F32)
+    out_rows = late_pieces[:, 208:272].reshape(16, 8, 8, 128).transpose(0, 2, 1, 3)
+    out_weight_grad = out_rows.reshape(128, 1024)
     return (
         result[None], input_grad[None], qkv_grad, out_weight_grad, gate_up_grad, down_grad,
         gain_grads[0], gain_grads[1],

time: 208 us -> 199 us (0.957)
  Pallas kernels: 194 us -> 187 us
  other arithmetic: 3.47 us -> 0.61 us
    pallas_call x1, Pallas kernels: 73.2 us -> 66.5 us  [backward(): pl.pallas_call(backward_kernel, name='backward', out_shape=(shape((128, 1...]
    convert_element_type x2 -> x1, other arithmetic: 3.01 us -> 0.19 us  [body(): down_grad = down_rows.reshape(328, 1024).astype(F32)]
    unnamed x13 -> x12, local copies, waits for them, and re-layouts: 5.86 us -> 5.3 us
where the time goes in v3:
time: 199 us
  Pallas kernels  187 us (94%)
  local copies, waits for them, and re-layouts  10.2 us (5%)
    pallas_call x1, Pallas kernels, front(): pl.pallas_call(front_kernel, name='front', out_shape=(shape((208, 1024)),...  121 us
    pallas_call x1, Pallas kernels, backward(): pl.pallas_call(backward_kernel, name='backward', out_shape=(shape((128, 1...  66.5 us
    unnamed x12, local copies, waits for them, and re-layouts  5.3 us

profile of v3, /device:TPU:1, one launch (start us, length us, event | category | flops | bytes accessed | tf_op | source)
XLA Modules:
  0.0 199.1 jit_solution(15209818156424593815)
XLA Ops:
  0.6 121.0 %front.1 = (bf16[208,1024]{1,0:T(8,128)(2,1)}, bf16[128,1024]{1,0:T(8,128)(2,1)}, f32[128,1024]{1,0:T(8,128)}, bf16[64,2048]{1,0:T(8,128)(2,1)}, bf16[704,128]{1...) custom-call(bf16[128,1024]{1,0:T(8,128)(2,1)} %bitcast.35, ...), custom_call_target="tpu_custom_call" | custom-call | tf_op jit(solution)/shard_map/front/pallas_call | solution.py:771
  121.6 66.5 %backward.1 = (bf16[128,1024]{1,0:T(8,128)(2,1)}, bf16[16,352,128]{2,1,0:T(8,128)(2,1)}, bf16[16,96,256]{2,1,0:T(8,128)(2,1)}, bf16[16,288,128]{2,1,0:T(8,128)(2,1)}) custom-call(bf16[2048,64]{1,0:T(8,128)(2,1)} %get-tuple-element.29.k_ref, bf16[2048,64]{1,0:T(8,128)(2,1)} %get-tuple-element.30.v_ref, bf16[64,2048]{1,0:T(8,128)(2,1)} %get-tuple-element.31.kt_ref, ...), custom_call_target="tpu_custom_call" | custom-call | tf_op jit(solution)/shard_map/backward/pallas_call | solution.py:979
  188.2 1.4 slice.30
  189.6 0.2 copy_convert_fusion
  189.8 0.0 copy-start.1
  189.8 2.3 %copy.25 = f32[128,5248]{1,0:T(8,128)} copy(f32[128,5248]{0,1:T(8,128)S(1)} %bitcast.30) | data formatting | bytes 5373952
  192.0 0.0 copy-done.1
  192.0 0.2 convert_bitcast_fusion
  192.2 0.0 copy-start
  192.2 1.8 copy.23
  194.1 0.0 copy-done
  194.1 0.1 slice.28
  194.2 0.2 copy.21
  194.4 1.6 copy.24
  196.0 0.0 copy-start.2
  196.0 0.2 convert_element_type.19
  196.3 0.0 copy-start.3
  196.3 0.8 slice_bitcast_fusion
  197.1 0.5 slice_bitcast_fusion.1
  197.7 0.0 copy-done.2
  197.7 0.7 copy.30
  198.4 0.0 copy-done.3
  198.4 0.7 copy.31
  (1 shorter events, 0.0 us)
Async XLA Ops:
  189.8 2.3 %copy-start.1 = (bf16[16,96,256]{2,1,0:T(8,128)(2,1)S(1)}, bf16[16,96,256]{2,1,0:T(8,128)(2,1)}, u32[]{:S(2)}) copy-start(bf16[16,96,256]{2,1,0:T(8,128)(2,1)} %get-tuple-element.47) | copy-start | bytes 2359300
  192.2 1.9 copy-start
  196.0 1.6 copy-start.2
  196.3 2.1 %copy-start.3 = (bf16[128,1024]{1,0:T(8,128)(2,1)S(1)}, bf16[128,1024]{1,0:T(8,128)(2,1)}, u32[]{:S(2)}) copy-start(bf16[128,1024]{1,0:T(8,128)(2,1)} %get-tuple-element.44) | copy-start | bytes 786436

commit v4 on v3

--- a/solution.py
+++ b/solution.py
@@ -443,6 +443,8 @@
 
 Q_BLOCK = 256
 UNITS = 352
+LATE = 288
+B = 155
 
 
 def pick_rows(select, matrix):
@@ -463,20 +465,24 @@
     return lax.broadcasted_iota(jnp.int32, dims, axis)
 
 
-def front_kernel(
+def layer_kernel(
     h_ref, dy_ref, wqkv_ref, wout_ref, wgu_ref, wdown_ref, g1_ref, g2_ref, cos_ref, sin_ref,
-    wq_ref, result_ref, dh1_ref, dot_ref, gusum_ref, gdown_ref, ggain_ref, gout_ref,
-    n1_ref, qt_out, kt_out, qr_out, kr_out, vr_out, ot_out, lse_out,
+    result_ref, dinput_ref, gupieces_ref, rowpieces_ref, latepieces_ref,
+    wq_ref, dh1, dout_t, gu_sum, gdown, ggain_two, gsum,
     hall, n1, dyall, nall, part, downsum, qt_ref, kt_ref, vt_ref, qr_ref, kr_ref, vr_ref, ot_ref, lse_ref,
     qkv_win, gu_acc, qkv_cols, gu_cols, down_rows, ob, att_ref, dat,
     woutall, gu_ref, downall, down_w, act, dgu, total, core_in, far, ggu, gu_along, gu_across, gu_keep,
-    h1_ref, down_total, core_down, far_down, send, recv, local,
+    h1_keep, down_total, core_down, far_down,
+    dproj, dk, dv, late, gu_pair, gu_mine, row_pair, row_mine, gout, row_sum, late_sum,
+    core_b, far_b, core_c, far_c, row_along, row_across, row_keep, late_along, late_across, late_keep,
+    send, recv, local,
 ):
     p = Place()
     links = Links(
         send, recv, on_ctx(p.other),
-        [hall.at[0], hall.at[0, pl.ds(0, 64)], qkv_cols, gu_cols, down_rows,
-         ob.at[:, pl.ds(0, 128)]],
+        [gu_keep, hall.at[0], hall.at[0, pl.ds(0, 64)], hall.at[0, pl.ds(0, 32)], qkv_cols, gu_cols,
+         down_rows, ob.at[:, pl.ds(0, 128)], gu_mine, gu_mine.at[pl.ds(0, 176)], row_mine,
+         row_mine.at[pl.ds(0, 48)], late_keep, late_keep.at[pl.ds(0, LATE // 2)]],
     )
     wins = [
         pltpu.make_async_copy(
@@ -551,7 +557,6 @@
         copy.start()
     gu_ref[:, lanes] = gu_cols[...]
     next(gather_out)
-    saves = []
 
     def project(b):
         gain = wq_ref[pl.ds(192, 1), :].astype(F32)
@@ -575,9 +580,6 @@
         qr_ref[at, :] = q.astype(F32).T.astype(BF16)
         kr_ref[at, :] = k.astype(F32).T.astype(BF16)
         vr_ref[at, :] = v.astype(F32).T.astype(BF16)
-        copy = pltpu.make_async_copy(n1.at[b], n1_ref.at[b], local.at[10 + len(saves)])
-        copy.start()
-        saves.append(copy)
 
     for b in ready:
         project(b)
@@ -634,15 +636,6 @@
         return 0
 
     lax.fori_loop(0, 8, attend, 0)
-    saves += [
-        pltpu.make_async_copy(src, dst, local.at[26 + n])
-        for n, (src, dst) in enumerate((
-            (qt_ref, qt_out), (kt_ref, kt_out), (qr_ref, qr_out), (kr_ref, kr_out),
-            (vr_ref, vr_out), (ot_ref, ot_out), (lse_ref, lse_out),
-        ))
-    ]
-    for copy in saves[16:]:
-        copy.start()
     others = [p.twin] + [p.planes[d] for d in (3, 1, 2)] + [p.twin_planes[d] for d in (3, 1, 2)]
     for i, f in enumerate(others):
         links.put(60 + i, out_half(f, p.k), out_half(f, p.k), on_ctx(p.other))
@@ -657,7 +650,7 @@
     gain = wq_ref[pl.ds(193, 1), :].astype(F32)
     att = att_ref[...].reshape(1024, 128)
     h1 = h_ref[...].astype(F32) + tn(att, woutall[...])
-    h1_ref[...] = h1
+    h1_keep[...] = h1
     xhat, _unused = normalize(h1)
     nall[p.t] = (xhat * gain).astype(BF16)
     gather = gather_column(p, links, 90, nall.at[p.t], nall, 128)
@@ -703,10 +696,10 @@
         g = nn(dgu[...], nall[:, :, cols].reshape(1024, 512))
         ggu[:, cols] = g.astype(BF16)
         ggain.append(jnp.sum(g * gu_ref[:, cols].astype(F32), axis=0, keepdims=True))
-    ggain_ref[...] = jnp.concatenate(ggain, axis=1) / gain
+    ggain_two[...] = jnp.concatenate(ggain, axis=1) / gain
     sum_gu = scatter_fsdp(
         p, links, 140, lambda f: ggu.at[:, lanes_of(f)], gu_along, gu_across, gu_keep,
-        gusum_ref, 2 * UNITS,
+        gu_sum, 2 * UNITS,
     )
     next(sum_gu)
     next(scatter)
@@ -718,7 +711,7 @@
     for half in range(2):
         cols = pl.ds(512 * half, 512)
         g = nn(act[...], dyall[:, :, cols].reshape(1024, 512)).astype(BF16)
-        gdown_ref[:, cols] = nn(spread, g).astype(BF16)
+        gdown[:, cols] = nn(spread, g).astype(BF16)
 
     def down(b, _):
         at = pl.ds(pl.multiple_of(b * 128, 128), 128)
@@ -729,126 +722,34 @@
     sum_down = scatter_column(p, links, 147, downsum, down_total, core_down, far_down, 128)
     next(sum_down)
     next(scatter, None)
-    h1 = h1_ref[...]
+    h1 = h1_keep[...]
     xhat, inv = normalize(h1)
     d_h1 = dy_ref[...].astype(F32) + norm_back(total[...], xhat, inv, gain)
-    dh1_ref[...] = d_h1
+    dh1[...] = d_h1
     d_h1_b = d_h1.astype(BF16)
     dat[...] = nt(woutall[...], d_h1_b).astype(BF16).reshape(16, 64, 128)
     lanes = pl.ds(pl.multiple_of(p.c * 128, 128), 128)
     for d in range(1, 16):
-        links.put(124 + d, dat.at[p.ring[d]], dot_ref.at[:, lanes], on_ctx(p.ring[d]))
-    dot_ref[:, lanes] = dat[p.c]
-    next(sum_down)
+        links.put(124 + d, dat.at[p.ring[d]], dout_t.at[:, lanes], on_ctx(p.ring[d]))
+    dout_t[:, lanes] = dat[p.c]
     att = att_ref[...]
     for g in range(4):
         rows = att[4 * g : 4 * g + 4].reshape(256, 128)
         block = nn(rows, d_h1_b).reshape(2, 16, 8, 1024).transpose(1, 0, 2, 3)
-        gout_ref[:, pl.ds(16 * g, 16), :] = block.reshape(16, 16, 1024).astype(BF16)
+        gsum[:, pl.ds(16 * g, 16), :] = block.reshape(16, 16, 1024).astype(BF16)
     next(sum_down)
-    next(sum_gu)
+
+    sum_out = scatter_ctx(p, links, B + 16, gsum, gout, core_b, far_b, 64)
+    next(sum_out)
     for d in range(1, 16):
-        links.got(124 + d, dot_ref.at[:, pl.ds(pl.multiple_of(p.ring[16 - d] * 128, 128), 128)])
-    next(sum_down, None)
-    result_ref[...] = (h1_ref[...] + down_total[...]).astype(BF16)
-    next(sum_gu, None)
-    for copy in saves:
-        copy.wait()
-    links.close()
-
-
-def shape(dims, dtype=BF16):
-    return jax.ShapeDtypeStruct(dims, dtype)
-
-
-def front(hidden, grad, wqkv, wout, wgu, wdown, g1, g2, cos, sin):
-    heads = [
-        shape((64, 2048)), shape((64, 2048)), shape((2048, 64)), shape((2048, 64)),
-        shape((2048, 64)), shape((64, 2048), F32), shape((1, 2048), F32),
-    ]
-    blocks = pltpu.VMEM((16, 128, 1024), BF16)
-    column = pltpu.VMEM((8, 128, 1024), BF16)
-    return pl.pallas_call(
-        front_kernel,
-        name="front",
-        out_shape=(
-            shape((208, 1024)), shape((128, 1024)), shape((128, 1024), F32),
-            shape((64, 2048)), shape((2 * UNITS, 128)), shape((384, 1024)),
-            shape((1, 1024), F32), shape((16, 64, 1024)), shape((16, 128, 1024)), *heads,
-        ),
-        in_specs=[VMEM, VMEM, ANY] + [VMEM] * 7,
-        out_specs=(VMEM,) * 8 + (ANY,) * 8,
-        scratch_shapes=[
-            blocks, blocks, column, column, column, column,
-            pltpu.VMEM((64, 2048), BF16),
-            pltpu.VMEM((64, 2048), BF16),
-            pltpu.VMEM((64, 2048), BF16),
-            pltpu.VMEM((2048, 64), BF16),
-            pltpu.VMEM((2048, 64), BF16),
-            pltpu.VMEM((2048, 64), BF16),
-            pltpu.VMEM((64, 2048), F32),
-            pltpu.VMEM((1, 2048), F32),
-            pltpu.VMEM((3, 128, 128), BF16),
-            pltpu.VMEM((UNITS, 128), F32),
-            pltpu.VMEM((208, 128), BF16),
-            pltpu.VMEM((2 * UNITS, 128), BF16),
-            pltpu.VMEM((48, 1024), BF16),
-            pltpu.VMEM((64, 2048), BF16),
-            pltpu.VMEM((16, 64, 128), BF16),
-            pltpu.VMEM((16, 64, 128), BF16),
-            pltpu.VMEM((1024, 1024), BF16),
-            pltpu.VMEM((2 * UNITS, 1024), BF16),
-            pltpu.VMEM((384, 1024), BF16),
-            pltpu.VMEM((UNITS, 1024), BF16),
-            pltpu.VMEM((UNITS, 1024), BF16),
-            pltpu.VMEM((2 * UNITS, 1024), BF16),
-            pltpu.VMEM((128, 1024), F32),
-        ] + column_scratch(128, 1024) + [pltpu.VMEM((2 * UNITS, 1024), BF16)]
-        + fsdp_scratch(2 * UNITS, 128)
-        + [pltpu.VMEM((128, 1024), F32), pltpu.VMEM((128, 1024), F32)]
-        + column_scratch(128, 1024) + [dma(155), dma(155), dma(33)],
-        compiler_params=params(1),
-    )(hidden, grad, wqkv, wout, wgu, wdown, g1, g2, cos, sin)
-
-
-LATE = 288
-
-
-def backward_kernel(
-    k_ref, v_ref, kt_ref, qt_ref, q_ref, dot_ref, ot_ref, lse_ref, cos_ref, sin_ref,
-    n1_ref, wq_ref, h_ref, dh1_ref, gu_sum, gdown_ref, ggain_ref, gout_ref,
-    dinput_ref, gupieces_ref, rowpieces_ref, latepieces_ref,
-    n1, gsum, dproj, dk, dv, part, late, gu_pair, gu_mine, row_pair, row_mine,
-    total, gout, row_sum, late_sum, *rest,
-):
-    (
-        core_b, far_b, core_c, far_c,
-        row_along, row_across, row_keep,
-        late_along, late_across, late_keep, send, recv, local,
-    ) = rest
-    p = Place()
-    links = Links(
-        send, recv, on_ctx(p.other),
-        [part.at[0], part.at[0, pl.ds(0, 64)], part.at[0, pl.ds(0, 32)], row_keep,
-         gu_mine, gu_mine.at[pl.ds(0, 176)], row_mine, row_mine.at[pl.ds(0, 48)], late_keep, late_keep.at[pl.ds(0, LATE // 2)]],
-    )
-    loads = [
-        pltpu.make_async_copy(gout_ref, gsum, local.at[5]),
-        pltpu.make_async_copy(n1_ref, n1, local.at[1]),
-    ]
-    for copy in loads:
-        copy.start()
-    greet(ctx_peers(p) + p.fsdp_peers)
-    loads[0].wait()
-    sum_out = scatter_ctx(p, links, 16, gsum, gout, core_b, far_b, 64)
-    next(sum_out)
+        links.got(124 + d, dout_t.at[:, pl.ds(pl.multiple_of(p.ring[16 - d] * 128, 128), 128)])
     sum_rows = scatter_fsdp(
-        p, links, 55, lambda f: gdown_ref.at[pl.ds(pl.multiple_of(f * 48, 16), 48)],
+        p, links, B + 55, lambda f: gdown.at[pl.ds(pl.multiple_of(f * 48, 16), 48)],
         row_along, row_across, row_keep, row_sum, 48,
     )
     next(sum_rows)
-    all_gu = gather_ctx(p, links, 69, gu_mine, gupieces_ref, UNITS)
-    mine = [
+    all_gu = gather_ctx(p, links, B + 69, gu_mine, gupieces_ref, UNITS)
+    mine_copies = [
         pltpu.make_async_copy(gu_mine, gupieces_ref.at[p.c], local.at[2]),
         pltpu.make_async_copy(row_mine, rowpieces_ref.at[p.c], local.at[3]),
         pltpu.make_async_copy(late_sum, latepieces_ref.at[p.c], local.at[4]),
@@ -859,38 +760,41 @@
     other_cols = pl.ds(pl.multiple_of(512 * (1 - p.xl), 128), 512)
     to_x = on_ctx(p.same("X"))
 
-    links.put(142, gu_sum.at[other_half], gu_pair, to_x)
+    def swap_gu():
+        next(sum_gu, None)
+        links.put(B + 142, gu_sum.at[other_half], gu_pair, to_x)
 
     def begin_gu():
-        links.got(142, gu_pair)
+        links.got(B + 142, gu_pair)
         add_rows(gu_mine, [(gu_sum.at[own_half], 0), (gu_pair, 0)], UNITS)
         next(all_gu)
 
     def swap_rows():
         next(sum_rows, None)
-        links.put(143, row_sum.at[:, other_cols], row_pair, to_x)
+        links.put(B + 143, row_sum.at[:, other_cols], row_pair, to_x)
 
     def step(stages):
         return lambda: next(stages, None)
 
     plan = {
-        0: [step(sum_out)], 1: [begin_gu], 3: [step(sum_out)], 4: [step(sum_out), step(sum_rows)],
-        5: [step(sum_out), step(all_gu)], 6: [step(sum_out), swap_rows], 7: [step(all_gu)],
+        0: [step(sum_out)], 1: [step(sum_gu), step(sum_down)], 2: [step(sum_out)],
+        3: [swap_gu, step(sum_down)], 4: [step(sum_out)], 5: [step(sum_out), begin_gu],
+        6: [step(sum_out), step(sum_rows)], 7: [step(all_gu), swap_rows],
     }
     dk[...] = jnp.zeros_like(dk)
     dv[...] = jnp.zeros_like(dv)
 
     def attend(i, _):
         at = pl.ds(pl.multiple_of(i * Q_BLOCK, Q_BLOCK), Q_BLOCK)
-        scores = nn(k_ref[...], qt_ref[:, at])
+        scores = nn(kr_ref[...], qt_ref[:, at])
         prob = jnp.exp(scores - lse_ref[:, at])
-        dout = dot_ref[:, at]
-        d_prob = nn(v_ref[...], dout)
+        dout = dout_t[:, at]
+        d_prob = nn(vr_ref[...], dout)
         delta = jnp.sum(dout.astype(F32) * ot_ref[:, at], axis=0, keepdims=True)
         d_scores = (prob * (d_prob - delta)).astype(BF16)
         d_query = nn(kt_ref[...], d_scores) * 0.125
         dproj[pl.ds(0, 64), at] = unrope_t(d_query, cos_ref[:, at], sin_ref[:, at]).astype(BF16)
-        dk[...] += nn(d_scores, q_ref[at, :])
+        dk[...] += nn(d_scores, qr_ref[at, :])
         dv[...] += nn(prob.astype(BF16), dout.astype(F32).T.astype(BF16))
         for n, steps in plan.items():
 
@@ -902,33 +806,35 @@
         return 0
 
     lax.fori_loop(0, 8, attend, 0)
+
+    result_ref[...] = (h1_keep[...] + down_total[...]).astype(BF16)
+    links.close(B)
 
     def project(b, _):
         at = pl.ds(pl.multiple_of(b * 128, 128), 128)
         d_key = unrope_t(dk[at, :].T, cos_ref[:, at], sin_ref[:, at])
         dproj[pl.ds(64, 64), at] = d_key.astype(BF16)
         dproj[pl.ds(128, 64), at] = dv[at, :].T.astype(BF16)
-        part[b] = tn(dproj[:, at], wq_ref[pl.ds(0, 192), :]).astype(BF16)
+        hall[b] = tn(dproj[:, at], wq_ref[pl.ds(0, 192), :]).astype(BF16)
         return 0
 
     lax.fori_loop(0, 16, project, 0)
     back = lockstep(
-        scatter_ctx(p, links, 32, part, total, core_c, far_c, 64, 0),
-        scatter_ctx(p, links, 126, part, total, core_c, far_c, 64, 64),
+        scatter_ctx(p, links, B + 32, hall, total, core_c, far_c, 64, 0),
+        scatter_ctx(p, links, B + 126, hall, total, core_c, far_c, 64, 64),
     )
     next(back)
     next(back)
     next(all_gu)
-    links.got(143, row_pair)
+    links.got(B + 143, row_pair)
     for half in range(2):
         own_lanes = pl.ds(pl.multiple_of(512 * p.xl + 256 * half, 128), 256)
         add_rows(
             row_mine.at[pl.ds(48 * half, 48)],
             [(row_sum.at[:, own_lanes], 0), (row_pair.at[:, pl.ds(256 * half, 256)], 0)], 48,
         )
-    all_rows = gather_ctx(p, links, 88, row_mine, rowpieces_ref, 96)
+    all_rows = gather_ctx(p, links, B + 88, row_mine, rowpieces_ref, 96)
     next(all_rows)
-    loads[1].wait()
     gain = wq_ref[pl.ds(192, 1), :].astype(F32)
     late[...] = jnp.zeros_like(late)
     ggain = []
@@ -940,7 +846,7 @@
     gain_row = jnp.concatenate(ggain, axis=1) / gain
     row = iota((16, 1024), 0)
     gains = jnp.where(row == 0, gain_row, 0.0)
-    late[pl.ds(192, 16), :] = jnp.where(row == 1, ggain_ref[...], gains).astype(BF16)
+    late[pl.ds(192, 16), :] = jnp.where(row == 1, ggain_two[...], gains).astype(BF16)
     for f in range(8):
         for g in range(4):
             pair = gout[pl.ds(8 * f, 8), pl.ds(256 * g, 256)]
@@ -948,7 +854,7 @@
                 [pair[:, :128], pair[:, 128:]], axis=0
             ).astype(BF16)
     sum_late = scatter_fsdp(
-        p, links, 62, lambda f: late.at[:, lanes_of(f)],
+        p, links, B + 62, lambda f: late.at[:, lanes_of(f)],
         late_along, late_across, late_keep, late_sum, LATE,
     )
     next(sum_late)
@@ -961,51 +867,22 @@
     next(all_gu)
     next(all_rows)
     next(sum_late, None)
-    all_late = gather_ctx(p, links, 107, late_sum, latepieces_ref, LATE)
+    all_late = gather_ctx(p, links, B + 107, late_sum, latepieces_ref, LATE)
     next(all_late)
     next(back, None)
     xhat, inv = normalize(h_ref[...].astype(F32))
     d_in = norm_back(total[...], xhat, inv, gain)
-    dinput_ref[...] = (dh1_ref[...] + d_in).astype(BF16)
-    for copy in mine:
+    dinput_ref[...] = (dh1[...] + d_in).astype(BF16)
+    for copy in mine_copies:
         copy.start()
     run_all([all_gu, all_late, all_rows])
-    for copy in mine:
+    for copy in mine_copies:
         copy.wait()
     links.close()
 
 
-def backward(*args):
-    return pl.pallas_call(
-        backward_kernel,
-        name="backward",
-        out_shape=(
-            shape((128, 1024)), shape((16, UNITS, 128)),
-            shape((16, 96, 256)), shape((16, LATE, 128)),
-        ),
-        in_specs=[VMEM] * 10 + [ANY] + [VMEM] * 6 + [ANY],
-        out_specs=(VMEM, ANY, ANY, ANY),
-        scratch_shapes=[
-            pltpu.VMEM((16, 128, 1024), BF16),
-            pltpu.VMEM((16, 64, 1024), BF16),
-            pltpu.VMEM((192, 2048), BF16),
-            pltpu.VMEM((2048, 64), F32),
-            pltpu.VMEM((2048, 64), F32),
-            pltpu.VMEM((16, 128, 1024), BF16),
-            pltpu.VMEM((LATE, 1024), BF16),
-            pltpu.VMEM((UNITS, 128), BF16),
-            pltpu.VMEM((UNITS, 128), BF16),
-            pltpu.VMEM((48, 512), BF16),
-            pltpu.VMEM((96, 256), BF16),
-            pltpu.VMEM((128, 1024), F32),
-            pltpu.VMEM((64, 1024), F32),
-            pltpu.VMEM((48, 1024), BF16),
-            pltpu.VMEM((LATE, 128), BF16),
-        ] + scatter_scratch(64, 1024) + scatter_scratch(128, 1024)
-        + fsdp_scratch(48, 1024) + fsdp_scratch(LATE, 128)
-        + [dma(144), dma(144), dma(6)],
-        compiler_params=params(3),
-    )(*args)
+def shape(dims, dtype=BF16):
+    return jax.ShapeDtypeStruct(dims, dtype)
 
 
 def fsdp_scratch(rows, cols):
@@ -1016,6 +893,46 @@
     ]
 
 
+def layer(*args):
+    blocks = pltpu.VMEM((16, 128, 1024), BF16)
+    column = pltpu.VMEM((8, 128, 1024), BF16)
+
+    def held(*dims, dtype=BF16):
+        return pltpu.VMEM(dims, dtype)
+
+    return pl.pallas_call(
+        layer_kernel,
+        name="layer",
+        out_shape=(
+            shape((128, 1024)), shape((128, 1024)), shape((16, UNITS, 128)),
+            shape((16, 96, 256)), shape((16, LATE, 128)),
+        ),
+        in_specs=[VMEM, VMEM, ANY] + [VMEM] * 7,
+        out_specs=(VMEM, VMEM, ANY, ANY, ANY),
+        scratch_shapes=[
+            held(208, 1024), held(128, 1024, dtype=F32), held(64, 2048), held(2 * UNITS, 128),
+            held(384, 1024), held(1, 1024, dtype=F32), held(16, 64, 1024),
+            blocks, blocks, column, column, column, column,
+            held(64, 2048), held(64, 2048), held(64, 2048),
+            held(2048, 64), held(2048, 64), held(2048, 64),
+            held(64, 2048, dtype=F32), held(1, 2048, dtype=F32),
+            held(3, 128, 128), held(UNITS, 128, dtype=F32), held(208, 128), held(2 * UNITS, 128),
+            held(48, 1024), held(64, 2048), held(16, 64, 128), held(16, 64, 128),
+            held(1024, 1024), held(2 * UNITS, 1024), held(384, 1024), held(UNITS, 1024),
+            held(UNITS, 1024), held(2 * UNITS, 1024), held(128, 1024, dtype=F32),
+            *column_scratch(128, 1024), held(2 * UNITS, 1024), *fsdp_scratch(2 * UNITS, 128),
+            held(128, 1024, dtype=F32), held(128, 1024, dtype=F32), *column_scratch(128, 1024),
+            held(192, 2048), held(2048, 64, dtype=F32), held(2048, 64, dtype=F32),
+            held(LATE, 1024), held(UNITS, 128), held(UNITS, 128), held(48, 512), held(96, 256),
+            held(64, 1024, dtype=F32), held(48, 1024), held(LATE, 128),
+            *scatter_scratch(64, 1024), *scatter_scratch(128, 1024),
+            *fsdp_scratch(48, 1024), *fsdp_scratch(LATE, 128),
+            dma(B + 144), dma(B + 144), dma(10),
+        ],
+        compiler_params=params(1),
+    )(*args)
+
+
 def nt(a, b):
     return lax.dot_general(a, b, (((1,), (1,)), ((), ())), preferred_element_type=F32)
 
@@ -1064,16 +981,9 @@
     hidden_b, grad_b = hidden_in[0], out_grad[0]
     cos, sin = rope_tables()
     cos, sin = jnp.asarray(cos), jnp.asarray(sin)
-    (
-        w_q, result, d_h1, do_t, gu_sum, g_down, g_gain_two, g_out,
-        n1, q_t, k_t, queries, keys, values, o_t, lse,
-    ) = front(
+    result, input_grad, gu_pieces, row_pieces, late_pieces = layer(
         hidden_b, grad_b, qkv_weight, out_weight, gate_up_weight, down_weight,
         attn_gain[None], mlp_gain[None], cos, sin,
-    )
-    input_grad, gu_pieces, row_pieces, late_pieces = backward(
-        keys, values, k_t, q_t, queries, do_t, o_t, lse, cos, sin,
-        n1, w_q, hidden_b, d_h1, gu_sum, g_down, g_gain_two, g_out,
     )
     late_pieces = late_pieces.astype(F32)
     qkv_grad = (

time: 199 us -> 191 us (0.960)
  Pallas kernels: 187 us -> 178 us
    pallas_call x2 -> x1, Pallas kernels: 187 us -> 178 us  [layer(): pl.pallas_call(layer_kernel, name='layer', out_shape=(shape((128, 1024)),...]
    unnamed x12 -> x14, local copies, waits for them, and re-layouts: 5.3 us -> 5.3 us
where the time goes in v4:
time: 191 us; the launch traced here: 190 us
  Pallas kernels  178 us (93%)
  local copies, waits for them, and re-layouts  8.9 us (5%)
  other arithmetic  1.98 us (1%)
    pallas_call x1, Pallas kernels, layer(): pl.pallas_call(layer_kernel, name='layer', out_shape=(shape((128, 1024)),...  178 us
    unnamed x14, local copies, waits for them, and re-layouts  5.3 us

profile of v4, /device:TPU:1, one launch (start us, length us, event | category | flops | bytes accessed | tf_op | source)
XLA Modules:
  0.0 190.0 jit_solution(12053795926101520755)
XLA Ops:
  0.6 178.4 %layer.1 = (bf16[128,1024]{1,0:T(8,128)(2,1)}, bf16[128,1024]{1,0:T(8,128)(2,1)}, bf16[16,352,128]{2,1,0:T(8,128)(2,1)}, bf16[16,96,256]{2,1,0:T(8,128)(2,1)}, bf16[16,288,128]{2,1,0:T(8,128)(2,1)}) custom-call(bf16[128,1024]{1,0:T(8,128)(2,1)} %bitcast.36, bf16[128,1024]{1,0:T(8,128)(2,1)} %bitcast.37, bf16[128,3072]{1,0:T(8,128)(2,1)} %wqkv_ref.1, ...), custom_call_target="tpu_custom_call" | custom-call | tf_op jit(solution)/shard_map/layer/pallas_call | solution.py:903
  179.1 0.0 copy-start
  179.1 1.6 convert_element_type.19
  180.7 0.5 slice_bitcast_fusion.1
  181.2 0.8 slice_bitcast_fusion
  182.1 0.0 copy-done
  182.1 0.1 slice.28
  182.2 0.2 copy.21
  182.4 0.0 copy-start.1
  182.4 1.6 copy.24
  184.0 0.0 copy-done.1
  184.0 0.1 slice.30
  184.1 0.2 copy_convert_fusion
  184.3 0.0 copy-start.2
  184.3 2.3 %copy.25 = f32[128,5248]{1,0:T(8,128)} copy(f32[128,5248]{0,1:T(8,128)S(1)} %bitcast.30) | data formatting | bytes 5373952
  186.6 0.0 copy-done.2
  186.6 0.2 convert_bitcast_fusion
  186.8 0.0 copy-start.4
  186.8 0.0 copy-start.3
  186.8 1.8 copy.23
  188.6 0.0 copy-done.4
  188.6 0.7 copy.30
  189.3 0.0 copy-done.3
  189.3 0.7 copy.31
  (1 shorter events, 0.0 us)
Async XLA Ops:
  179.1 3.0 %copy-start = (bf16[16,288,128]{2,1,0:T(8,128)(2,1)S(1)}, bf16[16,288,128]{2,1,0:T(8,128)(2,1)}, u32[]{:S(2)}) copy-start(bf16[16,288,128]{2,1,0:T(8,128)(2,1)} %get-tuple-element.15) | copy-start | bytes 3538948
  182.4 1.6 copy-start.1
  184.3 2.3 %copy-start.2 = (bf16[16,96,256]{2,1,0:T(8,128)(2,1)S(1)}, bf16[16,96,256]{2,1,0:T(8,128)(2,1)}, u32[]{:S(2)}) copy-start(bf16[16,96,256]{2,1,0:T(8,128)(2,1)} %get-tuple-element.17) | copy-start | bytes 2359300
  186.8 1.9 copy-start.4
  186.8 2.6 %copy-start.3 = (bf16[128,1024]{1,0:T(8,128)(2,1)S(1)}, bf16[128,1024]{1,0:T(8,128)(2,1)}, u32[]{:S(2)}) copy-start(bf16[128,1024]{1,0:T(8,128)(2,1)} %get-tuple-element.14) | copy-start | bytes 786436

commit v5 on v4

--- a/solution.py
+++ b/solution.py
@@ -218,9 +218,9 @@
     yield [cross["F"]]
 
 
-def scatter_column(p, links, base, part, total, core_in, far, rows):
+def scatter_column(p, links, base, part, total, core_in, far, rows, off=0):
     half = rows // 2
-    whole, top, bottom = pl.ds(0, rows), pl.ds(0, half), pl.ds(half, half)
+    whole, top, bottom = pl.ds(off, rows), pl.ds(off, half), pl.ds(off + half, half)
     to_p, to_m, to_k = on_ctx(p.same("P")), on_ctx(p.same("M")), on_ctx(p.other)
     order = ("F", "P", "M", "S")
     mid = [part.at[p.column[name]] for name in order]
@@ -232,32 +232,32 @@
         links.got(base + i, dst)
 
     for i, name in enumerate(order):
-        put(i, part.at[p.cross_column[name]], core_in.at[i], to_k)
+        put(i, part.at[p.cross_column[name], whole], core_in.at[i, whole], to_k)
     yield
 
     def pair(i):
-        got(i, core_in.at[i])
+        got(i, core_in.at[i, whole])
         return [(mid[i], 0), (core_in.at[i], 0)]
 
-    add_rows(mid[0], pair(0), rows)
+    add_rows(mid[0], pair(0), rows, off)
     put(4, mid[0].at[top], far.at[0, top], to_p)
     put(5, mid[0].at[bottom], far.at[0, bottom], to_m)
     yield
     terms = pair(1)
     got(4, far.at[0, top])
-    add_rows(mid[1], terms + [(far.at[0], 0)], half)
-    add_rows(mid[1], terms, half, half)
-    put(6, mid[1], far.at[1], to_p)
+    add_rows(mid[1], terms + [(far.at[0], 0)], half, off)
+    add_rows(mid[1], terms, half, off + half)
+    put(6, mid[1].at[whole], far.at[1, whole], to_p)
     terms = pair(2)
     got(5, far.at[0, bottom])
-    add_rows(mid[2], terms, half)
-    add_rows(mid[2], terms + [(far.at[0], 0)], half, half)
-    put(7, mid[2], far.at[2], to_m)
+    add_rows(mid[2], terms, half, off)
+    add_rows(mid[2], terms + [(far.at[0], 0)], half, off + half)
+    put(7, mid[2].at[whole], far.at[2, whole], to_m)
     yield
     terms = pair(3)
-    got(6, far.at[1])
-    got(7, far.at[2])
-    add_rows(total, terms + [(far.at[1], 0), (far.at[2], 0)], rows)
+    got(6, far.at[1, whole])
+    got(7, far.at[2, whole])
+    add_rows(total, terms + [(far.at[1], 0), (far.at[2], 0)], rows, off)
 
 
 def gather_fsdp(p, links, base, own, slot):
@@ -687,7 +687,10 @@
         waiting += found
         while len(waiting) > 1:
             feed(waiting.pop(0), waiting.pop(0))
-    scatter = scatter_column(p, links, 109, part, total, core_in, far, 128)
+    scatter = lockstep(
+        scatter_column(p, links, 109, part, total, core_in, far, 64, 0),
+        scatter_column(p, links, 117, part, total, core_in, far, 64, 64),
+    )
     next(scatter)
     next(scatter)
     ggain = []
@@ -777,9 +780,9 @@
         return lambda: next(stages, None)
 
     plan = {
-        0: [step(sum_out)], 1: [step(sum_gu), step(sum_down)], 2: [step(sum_out)],
-        3: [swap_gu, step(sum_down)], 4: [step(sum_out)], 5: [step(sum_out), begin_gu],
-        6: [step(sum_out), step(sum_rows)], 7: [step(all_gu), swap_rows],
+        0: [step(sum_out), step(sum_gu)], 1: [step(sum_down)], 2: [swap_gu, step(sum_out)],
+        3: [step(sum_down)], 4: [begin_gu, step(sum_out)], 5: [step(sum_out), step(sum_rows)],
+        6: [step(sum_out), step(all_gu), swap_rows], 7: [step(all_gu)],
     }
     dk[...] = jnp.zeros_like(dk)
     dv[...] = jnp.zeros_like(dv)
@@ -985,17 +988,16 @@
         hidden_b, grad_b, qkv_weight, out_weight, gate_up_weight, down_weight,
         attn_gain[None], mlp_gain[None], cos, sin,
     )
-    late_pieces = late_pieces.astype(F32)
     qkv_grad = (
         late_pieces[:, :192].reshape(16, 3, 64, 128).transpose(3, 1, 0, 2).reshape(128, 3072)
-    )
-    gain_grads = jnp.sum(late_pieces[:, 192:194], axis=0)
+    ).astype(F32)
+    gain_grads = jnp.sum(late_pieces[:, 192:194].astype(F32), axis=0)
     gate_up = gu_pieces.reshape(2, 8, UNITS, 128)[:, :, :328].transpose(0, 2, 1, 3)
     gate_up_grad = gate_up.reshape(5248, 128).astype(F32).T
     down_rows = row_pieces.reshape(2, 8, 2, 48, 256)[:, :, :, :41].transpose(3, 1, 0, 2, 4)
     down_grad = down_rows.reshape(328, 1024).astype(F32)
     out_rows = late_pieces[:, 208:272].reshape(16, 8, 8, 128).transpose(0, 2, 1, 3)
-    out_weight_grad = out_rows.reshape(128, 1024)
+    out_weight_grad = out_rows.reshape(128, 1024).astype(F32)
     return (
         result[None], input_grad[None], qkv_grad, out_weight_grad, gate_up_grad, down_grad,
         gain_grads[0], gain_grads[1],

time: 191 us -> 189 us (0.990)
  Pallas kernels: 178 us -> 176 us
    pallas_call x1, Pallas kernels: 178 us -> 176 us  [layer(): pl.pallas_call(layer_kernel, name='layer', out_shape=(shape((128, 1024)),...]
    unnamed x14 -> x12, local copies, waits for them, and re-layouts: 5.3 us -> 5.29 us
where the time goes in v5:
time: 189 us
  Pallas kernels  176 us (93%)
  local copies, waits for them, and re-layouts  9.1 us (5%)
  other arithmetic  2.94 us (2%)
    pallas_call x1, Pallas kernels, layer(): pl.pallas_call(layer_kernel, name='layer', out_shape=(shape((128, 1024)),...  176 us
    unnamed x12, local copies, waits for them, and re-layouts  5.29 us

profile of v5, /device:TPU:1, one launch (start us, length us, event | category | flops | bytes accessed | tf_op | source)
XLA Modules:
  0.0 188.8 jit_solution(10981986828930956876)
XLA Ops:
  0.6 176.1 %layer.1 = (bf16[128,1024]{1,0:T(8,128)(2,1)}, bf16[128,1024]{1,0:T(8,128)(2,1)}, bf16[16,352,128]{2,1,0:T(8,128)(2,1)}, bf16[16,96,256]{2,1,0:T(8,128)(2,1)}, bf16[16,288,128]{2,1,0:T(8,128)(2,1)}) custom-call(bf16[128,1024]{1,0:T(8,128)(2,1)} %bitcast.38, bf16[128,1024]{1,0:T(8,128)(2,1)} %bitcast.39, bf16[128,3072]{1,0:T(8,128)(2,1)} %wqkv_ref.1, ...), custom_call_target="tpu_custom_call" | custom-call | tf_op jit(solution)/shard_map/layer/pallas_call | solution.py:906
  176.7 0.8 convert_reduce_fusion
  177.5 0.5 slice_bitcast_fusion
  178.0 1.8 convert_bitcast_fusion.1
  179.8 1.2 slice.21
  181.0 0.2 copy.21
  181.2 0.0 copy-start
  181.2 1.6 copy.24
  182.8 0.0 copy-done
  182.8 0.1 slice.28
  182.9 0.2 copy_convert_fusion
  183.1 0.0 copy-start.1
  183.1 2.3 %copy.25 = f32[128,5248]{1,0:T(8,128)} copy(f32[128,5248]{0,1:T(8,128)S(1)} %bitcast.32) | data formatting | bytes 5373952
  185.3 0.0 copy-done.1
  185.3 0.2 convert_bitcast_fusion
  185.5 0.0 copy-start.3
  185.6 0.0 copy-start.2
  185.6 1.8 copy.23
  187.4 0.0 copy-done.3
  187.4 0.7 copy.30
  188.1 0.0 copy-done.2
  188.1 0.7 copy.31
Async XLA Ops:
  181.2 1.6 copy-start
  183.1 2.3 %copy-start.1 = (bf16[16,96,256]{2,1,0:T(8,128)(2,1)S(1)}, bf16[16,96,256]{2,1,0:T(8,128)(2,1)}, u32[]{:S(2)}) copy-start(bf16[16,96,256]{2,1,0:T(8,128)(2,1)} %get-tuple-element.17) | copy-start | bytes 2359300
  185.5 1.9 copy-start.3
  185.6 2.6 %copy-start.2 = (bf16[128,1024]{1,0:T(8,128)(2,1)S(1)}, bf16[128,1024]{1,0:T(8,128)(2,1)}, u32[]{:S(2)}) copy-start(bf16[128,1024]{1,0:T(8,128)(2,1)} %get-tuple-element.14) | copy-start | bytes 786436
